TPU v7x, 32 devices: a whole 2x2x4 slice. The times are simulated.
32 devices in a mesh: col: 8 (over z, x), row: 4 (over y, core).
Axes of the slice: x: 2, y: 2, z: 4, core: 2. Of those that a mesh axis runs over, the one named last changes fastest.
Arguments:
- trailing: float32 [12288, 4096], P('row', 'col'), may hold values from -6 to 6
- panel_rows: float32 [12288, 512], P(('row', 'col')), may hold values from -6 to 6
- pivot_block: float32 [512, 512], P('col'), as said below
- panel_fill: int32 [48, 2], replicated, may hold values 0 or 1
Outputs:
- updated: float32 [12288, 4096], P('row', 'col')
- panel_factor: float32 [12288, 512], P(('row', 'col'))
Inputs may be any that keep to these rules, and one draw needn't show every extreme that they name: `pivot_block`: Symmetric; each diagonal entry exceeds the sum of the magnitudes of the other entries of its row by at least 1. `panel_fill`: each entry is 1 with probability 0.15, independently of the others.
All inputs are finite; a program needn't handle non-finite values.
Results may differ from a plain program's by a relative error of at most 0.00008.
Values sent between devices are 32-bit elements; how exact they have to be, the bound alone decides.
No kernel may reach another device: no remote copies, remote signals or barrier semaphores. Data moves between devices by JAX's collectives and lax.ppermute only.
A program may use at most 128 MiB of HBM per device.

v0:
```python
import functools
import math

import jax
import jax.numpy as jnp
from jax import lax
from jax.experimental import pallas as pl
from jax.experimental.pallas import tpu as pltpu
from jax.sharding import PartitionSpec as P

F32, BF16 = jnp.float32, jnp.bfloat16
VMEM = pl.BlockSpec(memory_space=pltpu.VMEM)
SMEM = pl.BlockSpec(memory_space=pltpu.SMEM)
HBM = pl.BlockSpec(memory_space=pltpu.HBM)
COARSE_STEPS = 2
FINE_STEPS = 16
RESIDUAL = 5e-4
STAGES = 8


def halves(value):
    high = value.astype(BF16)
    return high, (value - high.astype(F32)).astype(BF16)


def dot(a, b, dims):
    return lax.dot_general(a, b, (dims, ((), ())), preferred_element_type=F32)


NN, NT, TN = ((1,), (0,)), ((1,), (1,)), ((0,), (0,))


def dot3(a, b, dims):
    (ah, al), (bh, bl) = a, b
    return dot(ah, bh, dims) + (dot(ah, bl, dims) + dot(al, bh, dims))


def inverse_factor_kernel(where_ref, *refs):
    parts, (w_ref, s_ref) = refs[:-2], refs[-2:]
    n = w_ref.shape[0]
    pieces, share = parts[0].shape[0], parts[0].shape[1]
    own = where_ref[1] % len(parts)
    for flip, ref in enumerate(parts):
        at = jnp.bitwise_xor(own, flip) * share
        for i in range(pieces):
            s_ref[pl.ds(pl.multiple_of(i * len(parts) * share + at, share), share), :] = ref[i]
    rows = lax.broadcasted_iota(jnp.int32, (n, n), 0)
    cols = lax.broadcasted_iota(jnp.int32, (n, n), 1)
    eye = (rows == cols).astype(F32)
    take = jnp.where(rows > cols, 1.0, 0.5 * eye)
    a = s_ref[...]
    diag_row = jnp.sum(a * eye, axis=0, keepdims=True)
    diag_col = jnp.sum(a * eye, axis=1, keepdims=True)
    scale_row, scale_col = lax.rsqrt(diag_row), lax.rsqrt(diag_col)
    scaled = jnp.where(rows == cols, 1.0, a * scale_row * scale_col)
    s_ref[...] = scaled
    scaled_parts = halves(scaled)
    w = eye - take * (scaled - eye)
    for _ in range(COARSE_STEPS):
        wh = w.astype(BF16)
        t = dot(wh, scaled_parts[0], NN).astype(BF16)
        change = take * (dot(t, wh, NT) - eye)
        w = w - dot(change.astype(BF16), wh, NN)
    w_ref[...] = w

    def fine(state):
        step, _ = state
        w = w_ref[...]
        parts = halves(w)
        t = halves(dot3(parts, halves(s_ref[...]), NN))
        residual = dot3(t, parts, NT) - eye
        w_ref[...] = w - dot((take * residual).astype(BF16), parts[0], NN)
        return step + 1, jnp.sum(residual * residual)

    _, left = lax.while_loop(
        lambda state: jnp.logical_and(state[0] < FINE_STEPS, jnp.logical_not(state[1] < RESIDUAL**2)),
        fine,
        (jnp.int32(0), jnp.float32(1.0)),
    )
    done = left < RESIDUAL**2

    @pl.when(jnp.logical_not(done))
    def _():
        w_ref[...] = eye

        def eliminate(j, carry):
            row = s_ref[pl.ds(j, 1), :]
            pick = lax.broadcasted_iota(jnp.int32, (1, n), 1) == j
            pivot = jnp.sum(jnp.where(pick, row, 0.0), axis=1, keepdims=True)
            column = jnp.sum(jnp.where(pick, s_ref[...], 0.0), axis=1, keepdims=True)
            below = lax.broadcasted_iota(jnp.int32, (n, 1), 0) > j
            ratio = jnp.where(below, column / pivot, 0.0)
            s_ref[...] = s_ref[...] - ratio * row
            w_ref[...] = w_ref[...] - ratio * w_ref[pl.ds(j, 1), :]
            return carry

        lax.fori_loop(0, n, eliminate, 0)
        pivots = jnp.sum(s_ref[...] * eye, axis=1, keepdims=True)
        w_ref[...] = w_ref[...] * lax.rsqrt(pivots)

    w_ref[...] = w_ref[...] * scale_row


def inverse_factor(where, parts):
    n = parts[0].shape[-1]
    return pl.pallas_call(
        inverse_factor_kernel,
        out_shape=jax.ShapeDtypeStruct((n, n), F32),
        in_specs=[SMEM] + [VMEM] * len(parts),
        out_specs=VMEM,
        scratch_shapes=[pltpu.VMEM((n, n), F32)],
        compiler_params=pltpu.CompilerParams(vmem_limit_bytes=20 * 2**20),
    )(where, *parts)


class Sizes:
    def __init__(self, trailing, panel_rows, panel_fill):
        self.cols, self.rows = lax.axis_size("col"), lax.axis_size("row")
        self.block = panel_rows.shape[1] // 2
        self.piece = panel_rows.shape[0]
        self.unit = math.gcd(self.piece, self.block)
        self.per_piece = self.piece // self.unit
        self.per_block = self.block // self.unit
        self.slab = self.piece * self.cols
        self.merge = self.per_block if 2 * self.piece % self.block == 0 else 1
        self.width = trailing.shape[1]
        self.tiles = self.cols * self.per_piece

        self.groups = self.cols // 2
        self.column_units = 2 * self.width // self.unit
        self.needed = sorted({s for g in range(self.groups) for s in self.shifts(g)})

    def pair_slab(self, group):
        return 2 * group * self.width // self.slab

    def pair_start(self, group):
        return (2 * group * self.width - self.pair_slab(group) * self.slab) // self.unit

    def shifts(self, group):
        start = self.pair_start(group) * self.unit
        first, last = start // (2 * self.piece), (start + 2 * self.width - 1) // (2 * self.piece)
        return [(g - group) % self.groups for g in range(first, last + 1)]


def unit_flag(sizes, fill_ref, piece_index, unit, panel):
    block = (piece_index * sizes.per_piece + unit) // sizes.per_block
    return fill_ref[block * 2 + panel] != 0


def pool_pieces(sizes, pool_row, pool_col):
    for core in range(2):
        for side in range(2):
            yield core, side, (pool_row * 2 + core) * sizes.cols + pool_col * 2 + side


def pair_flag(sizes, fill_ref, group, index):
    unit = sizes.pair_slab(group) * sizes.tiles + sizes.pair_start(group) + index // 2
    return fill_ref[unit // sizes.per_block * 2 + index % 2] != 0


def level_kernel(sizes, levels, fill_ref, out_ref):
    pool_most, column_most = jnp.int32(0), jnp.int32(0)
    for pool_row in range(sizes.rows // 2):
        for pool_col in range(sizes.groups):
            count = jnp.int32(0)
            for _, _, piece in pool_pieces(sizes, pool_row, pool_col):
                for u in range(sizes.per_piece):
                    for p in range(2):
                        count = count + unit_flag(sizes, fill_ref, piece, u, p).astype(jnp.int32)
            pool_most = jnp.maximum(pool_most, count)
    for group in range(sizes.groups):
        for side in range(2):
            count = jnp.int32(0)
            for i in range(sizes.column_units):
                flag = pair_flag(sizes, fill_ref, group, side * sizes.column_units + i)
                count = count + flag.astype(jnp.int32)
            column_most = jnp.maximum(column_most, count)
    level = jnp.int32(0)
    for cap, column_cap in levels[:-1]:
        fits = jnp.logical_and(pool_most <= cap, column_most <= column_cap)
        level = level + jnp.logical_not(fits).astype(jnp.int32)
    out_ref[0] = level


def level_of(sizes, levels, fill):
    return pl.pallas_call(
        functools.partial(level_kernel, sizes, levels),
        out_shape=jax.ShapeDtypeStruct((1,), jnp.int32),
        in_specs=[SMEM],
        out_specs=SMEM,
    )(fill)


def pack_kernel(sizes, cap, where_ref, fill_ref, panel_ref, core_ref, side_ref, out_ref, pool):
    c, r = where_ref[0], where_ref[1]
    side, core = c % 2, r % 2
    quarter = sizes.unit // 4
    own_at = pl.multiple_of((side * 2 + core) * quarter, quarter)
    for u in range(sizes.per_piece):
        pool[core, side, u] = panel_ref[u, pl.ds(own_at, quarter), :]
        pool[1 - core, side, u] = core_ref[u, side]
        pool[core, 1 - side, u] = side_ref[0, u]
        pool[1 - core, 1 - side, u] = side_ref[1, u]
    slot = jnp.int32(0)
    for core_at, side_at, piece in pool_pieces(sizes, r // 2, c // 2):
        for u in range(sizes.per_piece):
            for p in range(2):
                flag = unit_flag(sizes, fill_ref, piece, u, p)

                @pl.when(flag)
                def _(slot=slot, core_at=core_at, side_at=side_at, u=u, p=p):
                    out_ref[jnp.minimum(slot, cap - 1)] = pool[
                        core_at, side_at, u, :, p * sizes.block : (p + 1) * sizes.block
                    ]

                slot = slot + flag.astype(jnp.int32)


def pack(sizes, cap, where, fill, panel, from_core, from_side):
    quarter = sizes.unit // 4
    return pl.pallas_call(
        functools.partial(pack_kernel, sizes, cap),
        out_shape=jax.ShapeDtypeStruct((cap, quarter, sizes.block), F32),
        in_specs=[SMEM, SMEM, VMEM, VMEM, VMEM],
        out_specs=VMEM,
        scratch_shapes=[pltpu.VMEM((2, 2, sizes.per_piece, quarter, 2 * sizes.block), F32)],
        compiler_params=pltpu.CompilerParams(vmem_limit_bytes=16 * 2**20),
    )(where, fill, panel, from_core, from_side)


def pair_slots(sizes, fill_ref, group, slots):
    def step(i, slot):
        flag = pair_flag(sizes, fill_ref, group, i)
        slot = jnp.where(i == sizes.column_units, 0, slot)
        slots[i] = jnp.where(flag, slot, -1)
        return slot + flag.astype(jnp.int32)

    lax.fori_loop(0, 2 * sizes.column_units, step, jnp.int32(0))


def pack_column_kernel(sizes, cap, column_cap, shifts, where_ref, fill_ref, *refs):
    lists, before, (out_ref, slots) = refs[: len(shifts)], refs[len(shifts) : -2], refs[-2:]
    own = where_ref[0] // 2
    slab, start = sizes.pair_slab(own), sizes.pair_start(own)
    pair_slots(sizes, fill_ref, own, slots)
    for ref in before:
        out_ref[...] = ref[...]
    for shift, list_ref in zip(shifts, lists):
        group = lax.rem(own + shift, sizes.groups)
        slot = jnp.int32(0)
        for core, side, piece in pool_pieces(sizes, slab // 2, group):
            for u in range(sizes.per_piece):
                for p in range(2):
                    flag = unit_flag(sizes, fill_ref, piece, u, p)
                    index = (((group * 2 + side) * sizes.per_piece + u) - start) * 2 + p
                    inside = jnp.logical_and(index >= 0, index < 2 * sizes.column_units)
                    wanted = jnp.logical_and(jnp.logical_and(flag, inside), slab % 2 == core)

                    @pl.when(wanted)
                    def _(slot=slot, index=index, list_ref=list_ref):
                        index = jnp.clip(index, 0, 2 * sizes.column_units - 1)
                        target = jnp.clip(slots[index], 0, column_cap - 1)
                        out_ref[index // sizes.column_units, target] = list_ref[jnp.minimum(slot, cap - 1)]

                    slot = slot + flag.astype(jnp.int32)


def pack_column(sizes, cap, column_cap, shifts, where, fill, lists, before=()):
    return pl.pallas_call(
        functools.partial(pack_column_kernel, sizes, cap, column_cap, shifts),
        out_shape=jax.ShapeDtypeStruct((2, column_cap, sizes.unit // 4, sizes.block), F32),
        in_specs=[SMEM, SMEM] + [VMEM] * (len(lists) + len(before)),
        out_specs=VMEM,
        scratch_shapes=[pltpu.SMEM((2 * sizes.column_units,), jnp.int32)],
        compiler_params=pltpu.CompilerParams(vmem_limit_bytes=20 * 2**20),
    )(where, fill, *lists, *before)


def own_factor_kernel(sizes, where_ref, fill_ref, w_ref, panel_ref, window_ref, x_ref, slot_ref, near_ref, inverse_ref, masked, sem, sems):
    c, r = where_ref[0], where_ref[1]
    rows = window_ref.shape[0] // STAGES
    stages = []
    for i in range(STAGES):
        at = pl.ds(i * rows, rows)
        stages.append(pltpu.make_async_copy(window_ref.at[at], near_ref.at[at], sems.at[i]))
        stages[i].start()
    own = r * sizes.cols + c
    for u in range(sizes.per_piece):
        for p in range(2):
            at = (pl.ds(u * sizes.unit, sizes.unit), pl.ds(p * sizes.block, sizes.block))
            masked[at] = jnp.where(unit_flag(sizes, fill_ref, own, u, p), panel_ref[at], 0.0)
    w = halves(w_ref[...])
    masked[...] = dot3(halves(masked[...]), w, NT)
    copy_out = pltpu.make_async_copy(masked, x_ref, sem)
    copy_out.start()
    inverse_ref[...] = dot3(w, w, TN)

    @pl.loop(0, sizes.groups)
    def _(shift):
        group = lax.rem(c // 2 + shift, sizes.groups)
        slot = jnp.int32(0)
        for core, side, piece in pool_pieces(sizes, r // 2, group):
            for u in range(sizes.per_piece):
                for p in range(2):
                    flag = unit_flag(sizes, fill_ref, piece, u, p)

                    @pl.when(core == r % 2)
                    def _(slot=slot, flag=flag, side=side, u=u, p=p):
                        at = ((shift * 2 + side) * sizes.per_piece + u) * 2 + p
                        slot_ref[at] = jnp.where(flag, slot, -1)

                    slot = slot + flag.astype(jnp.int32)

    copy_out.wait()
    for stage in stages:
        stage.wait()


def own_factor(sizes, where, fill, w, panel, window):
    return pl.pallas_call(
        functools.partial(own_factor_kernel, sizes),
        out_shape=(
            pltpu.HBM(panel.shape, F32),
            jax.ShapeDtypeStruct((2 * sizes.tiles,), jnp.int32),
            pltpu.VMEM(window.shape, F32),
            jax.ShapeDtypeStruct(w.shape, F32),
        ),
        in_specs=[SMEM, SMEM, VMEM, VMEM, HBM],
        out_specs=(HBM, SMEM, VMEM, VMEM),
        scratch_shapes=[
            pltpu.VMEM(panel.shape, F32),
            pltpu.SemaphoreType.DMA,
            pltpu.SemaphoreType.DMA((STAGES,)),
        ],
        compiler_params=pltpu.CompilerParams(vmem_limit_bytes=20 * 2**20),
    )(where, fill, w, panel, window)


def column_factor_kernel(sizes, where_ref, fill_ref, inverse_ref, *refs):
    lists, (out_ref, column, slots) = refs[:4], refs[4:]
    c, r = where_ref[0], where_ref[1]
    side, core = c % 2, r % 2
    quarter = sizes.unit // 4
    pair_slots(sizes, fill_ref, c // 2, slots)
    column[...] = jnp.zeros_like(column)

    @pl.loop(0, sizes.column_units // 2)
    def _(unit):
        for p in range(2):
            slot = slots[side * sizes.column_units + unit * 2 + p]

            @pl.when(slot >= 0)
            def _(slot=slot, p=p):
                for flip in range(4):
                    from_side = jnp.bitwise_xor(side, flip // 2)
                    from_core = jnp.bitwise_xor(core, flip % 2)
                    at = pl.multiple_of(unit * sizes.unit + (from_side * 2 + from_core) * quarter, quarter)
                    column[pl.ds(at, quarter), pl.ds(p * sizes.block, sizes.block)] = lists[flip][slot]

    out_ref[...] = dot3(halves(inverse_ref[...]), halves(column[...]), NT)


def column_factor(sizes, where, fill, inverse, lists):
    n = inverse.shape[0]
    return pl.pallas_call(
        functools.partial(column_factor_kernel, sizes),
        out_shape=jax.ShapeDtypeStruct((n, sizes.width), F32),
        in_specs=[SMEM, SMEM, VMEM] + [VMEM] * 4,
        out_specs=VMEM,
        scratch_shapes=[pltpu.VMEM((sizes.width, n), F32), pltpu.SMEM((2 * sizes.column_units,), jnp.int32)],
        compiler_params=pltpu.CompilerParams(vmem_limit_bytes=20 * 2**20),
    )(where, fill, inverse, *lists)


def update_kernel(sizes, counts, where_ref, slot_ref, column_ref, window_ref, *refs):
    groups, merge = sizes.groups, sizes.merge
    refs, (out_ref, tiles, data, right, out_sems) = list(refs[:-5]), refs[-5:]
    lists = []
    for count in counts:
        own, other, *cores = [refs.pop(0) for _ in range(count)]
        cores = cores if count == 4 else [cores[0].at[0], cores[0].at[1]]
        lists += [own, cores[0], other, cores[1]]
    c, r = where_ref[0], where_ref[1]
    side, core = c % 2, r % 2
    per_group = 2 * sizes.per_piece // merge
    rows = merge * sizes.unit
    quarter = sizes.unit // 4

    def rows_of(t):
        group = lax.rem(c // 2 + t // per_group, groups)
        return pl.ds(pl.multiple_of((group * per_group + t % per_group) * rows, rows), rows)

    def tile_out(t, source):
        return pltpu.make_async_copy(source, out_ref.at[rows_of(t)], out_sems.at[t])

    def slot_of(t, p, part):
        return slot_ref[(t * merge + part) * 2 + p]

    def active(t):
        return jnp.logical_or(slot_of(t, 0, 0) >= 0, slot_of(t, 1, 0) >= 0)

    @pl.loop(0, per_group * groups)
    def _(t):
        pl.when(jnp.logical_not(active(t)))(tile_out(t, window_ref.at[rows_of(t)]).start)

    for p in range(2):
        high, low = halves(column_ref[p * sizes.block : (p + 1) * sizes.block, :])
        for i, part in enumerate((high, low, high)):
            right[p, i * sizes.block : (i + 1) * sizes.block, :] = part

    for group in range(groups):

        @pl.loop(group * per_group, (group + 1) * per_group)
        def _(t, group=group):
            @pl.when(active(t))
            def _():
                tiles[t] = window_ref[rows_of(t), :]
                for p in range(2):

                    @pl.when(slot_of(t, p, 0) >= 0)
                    def _(p=p):
                        for part in range(merge):
                            slot = slot_of(t, p, part)
                            for flip in range(4):
                                from_side = jnp.bitwise_xor(side, flip // 2)
                                from_core = jnp.bitwise_xor(core, flip % 2)
                                at = pl.multiple_of((part * 4 + from_side * 2 + from_core) * quarter, quarter)
                                data[pl.ds(at, quarter), :] = lists[4 * group + flip][slot]
                        high, low = halves(data[...])
                        left = jnp.concatenate([high, high, low], axis=1)
                        tiles[t] = tiles[t] - dot(left, right[p], NN)

                tile_out(t, tiles.at[t]).start()

    @pl.loop(0, per_group * groups)
    def _(t):
        tile_out(t, tiles.at[t]).wait()


def update(sizes, where, slots, column, window, lists):
    rows = sizes.merge * sizes.unit
    tiles = sizes.slab // rows
    list_bytes = 4 * sum(value.size for group in lists for value in group)
    return pl.pallas_call(
        functools.partial(update_kernel, sizes, [len(group) for group in lists]),
        out_shape=pltpu.HBM(window.shape, F32),
        in_specs=[SMEM, SMEM, VMEM, VMEM] + [VMEM] * sum(len(group) for group in lists),
        out_specs=HBM,
        scratch_shapes=[
            pltpu.VMEM((tiles, rows, sizes.width), F32),
            pltpu.VMEM((rows, sizes.block), F32),
            pltpu.VMEM((2, 3 * sizes.block, sizes.width), BF16),
            pltpu.SemaphoreType.DMA((tiles,)),
        ],
        compiler_params=pltpu.CompilerParams(vmem_limit_bytes=14 * 2**20 + list_bytes),
    )(where, slots, column, window, *(value for group in lists for value in group))


def swap(value, axis, step):
    size = lax.axis_size(axis)
    return lax.ppermute(value, axis, [(i, i ^ step) for i in range(size)])


def join(index, step, own, other):
    second = (index & step) != 0
    return jnp.where(second, jnp.concatenate([other, own], 0), jnp.concatenate([own, other], 0))


def after(value, *earlier):
    return lax.optimization_barrier((value, *earlier))[0]


def bring(sizes, value, shift):
    pairs = [(i, (i - 2 * shift) % sizes.cols) for i in range(sizes.cols)]
    return lax.ppermute(value, "col", pairs)


def spread_column(sizes, value, step):
    r, c = lax.axis_index("row"), lax.axis_index("col")
    pairs = []
    for at in range(sizes.cols):
        slab = sizes.pair_slab(at // 2)
        for row in range(sizes.rows):
            if (row // 2 ^ slab // 2) % step == 0:
                pairs.append((at * sizes.rows + row, at * sizes.rows + (row ^ step)))
    other = lax.ppermute(value, ("col", "row"), pairs)
    return jnp.where(((r ^ sizes.pair_slab(c // 2)) & step) != 0, other, value)


def per_device(trailing, panel_rows, pivot_block, panel_fill):
    sizes = Sizes(trailing, panel_rows, panel_fill)
    fill = panel_fill.reshape(-1)
    r, c = lax.axis_index("row"), lax.axis_index("col")
    where = jnp.stack([c, r]).astype(jnp.int32)
    side, core = c % 2, r % 2
    quarter = sizes.unit // 4
    split = min(4, pivot_block.shape[0] // 8)
    share = pivot_block.shape[0] // split
    most, column_most = 8 * sizes.per_piece, sizes.column_units
    levels = [(most * 5 // 12, column_most * 3 // 4), (most, column_most)]

    units = panel_rows.reshape(sizes.per_piece, sizes.unit, -1)
    quarters = panel_rows.reshape(sizes.per_piece, 2, 2, quarter, -1)

    def at_core(which):
        return lax.dynamic_index_in_dim(quarters, which, 2, keepdims=False)

    pivot = lax.dynamic_slice_in_dim(pivot_block, r % split * share, share, 0)[None]
    pivot = join(c, 1, pivot, swap(pivot, "col", 1))
    from_core = swap(at_core(1 - core), "row", 1)
    from_core, pivot = lax.optimization_barrier((from_core, pivot))
    both = jnp.stack([at_core(core), from_core])
    from_side = swap(lax.dynamic_index_in_dim(both, 1 - side, 2, keepdims=False), "col", 1)
    step = 2
    while step < sizes.cols:
        pivot = join(c, step, pivot, swap(pivot, "col", step))
        step *= 2

    def run(cap, column_cap, trailing, panel_rows, fill, units, from_core, from_side, pivot):
        own = pack(sizes, cap, where, fill, units, from_core, from_side)
        lists = {0: own}
        first = [s for s in range(1, sizes.groups) if s in sizes.needed]
        later = [s for s in range(1, sizes.groups) if s not in sizes.needed]
        lists |= {s: bring(sizes, own, s) for s in first}
        sides = {0: swap(own, "col", 1)}
        parts = [pivot] + ([swap(pivot, "row", 2)] if split == 4 else [])
        parts = [part for value in parts for part in (value, swap(value, "row", 1))]
        near = first[0]
        lists[near], *parts = lax.optimization_barrier((lists[near], *parts))
        sides[near] = swap(lists[near], "col", 1)
        w = inverse_factor(where, parts)
        soon, rest = [0, near], [s for s in sizes.needed if s not in (0, near)]
        column = pack_column(sizes, cap, column_cap, soon, where, fill, [lists[s] for s in soon])
        held = lax.optimization_barrier((w, column, sides[0], sides[near], *lists.values()))
        w, column, sides[0], sides[near] = held[:4]
        lists = dict(zip(lists, held[4:]))

        column = pack_column(sizes, cap, column_cap, rest, where, fill, [lists[s] for s in rest], [column])
        lists |= {s: bring(sizes, lists[0], s) for s in later}
        sides |= {s: swap(lists[s], "col", 1) for s in first[1:]}
        step = sizes.rows // 2
        while step > 1:
            column = spread_column(sizes, column, step)
            step //= 2
        panel_factor, slots, window, inverse = own_factor(sizes, where, fill, w, panel_rows, trailing)
        column, slots = lax.optimization_barrier((column, slots))
        across = swap(lax.dynamic_index_in_dim(column, 1 - side, 0, keepdims=False), "col", 1)
        column = lax.dynamic_index_in_dim(column, side, 0, keepdims=False)
        columns = [column, swap(column, "row", 1), across, swap(across, "row", 1)]
        for s in later:
            lists[s] = lax.optimization_barrier((lists[s], slots, *(sides[j] for j in first)))[0]
            sides[s] = swap(lists[s], "col", 1)
        column = column_factor(sizes, where, fill, inverse, columns)
        for s in later:
            sides[s], column = lax.optimization_barrier((sides[s], column))
        ordered = []
        for s in range(sizes.groups):
            value, other = lists[s], sides[s]
            if s in later:
                ordered.append((value, other, swap(value, "row", 1), swap(other, "row", 1)))
            else:
                ordered.append((value, other, swap(jnp.stack([value, other]), "row", 1)))
        return update(sizes, where, slots, column, window, ordered), panel_factor

    operands = (trailing, panel_rows, fill, units, from_core, from_side, pivot)
    branches = [functools.partial(run, *level) for level in levels]
    return lax.cond(level_of(sizes, levels, fill)[0] == 0, *branches, *operands)


def solution(mesh):
    in_specs = (P("row", "col"), P(("row", "col"), None), P("col", None), P())
    out_specs = (P("row", "col"), P(("row", "col"), None))
    return jax.shard_map(
        per_device, mesh=mesh, in_specs=in_specs, out_specs=out_specs, check_vma=False
    )
```

profile of v0, /device:TPU:0, one launch (start us, length us, event | category | flops | bytes accessed | tf_op | source)
XLA Modules:
  0.0 79.4 jit_solution(183640526867481558)
XLA Ops:
  0.6 0.0 copy-start
  0.7 1.2 %dynamic-slice_bitcast_fusion.4 = (f32[1,3,2,32,512]{4,3,2,1,0:T(8,128)S(1)}, f32[3,2,32,512]{3,2,1,0:T(8,128)S(1)}) fusion(f32[3,2,2,32,512]{4,3,2,1,0:T(8,128)} %bitcast.50, s32[]{:T(128)S(6)} %select_n.102, s32[]{:T(128)S(6)} %select_n.97), kind=kLoop, calls=%fused_computation.18 | loop fusion | bytes 1572872 | tf_op jit(solution)/shard_map/stack | solution.py:512
  1.9 0.0 copy-start.6
  1.9 0.5 collective-permute-start.38
  2.5 2.6 %collective-permute-start.39 = (f32[1,16,512]{2,1,0:T(8,128)S(1)}, f32[1,16,512]{2,1,0:T(8,128)S(1)}, u32[]{:S(2)}, u32[]{:S(2)}) collective-permute-start(f32[1,16,512]{2,1,0:T(8,128)S(1)} %dynamic-slice_bitcast_fusion.6), channel_id=1, source_target_pairs={{0,4},{4,0},{8,12},{12,8},{16,20},{20,16},{24,28},{28,24},{1,5},{5... | collective-permute-start | bytes 98312 | tf_op jit(solution)/shard_map/ppermute | solution.py:461
  5.1 1.9 %collective-permute-done.39 = f32[1,16,512]{2,1,0:T(8,128)S(1)} collective-permute-done((f32[1,16,512]{2,1,0:T(8,128)S(1)}, f32[1,16,512]{2,1,0:T(8,128)S(1)}, u32[]{:S(2)}, u32[]{:S(2)}) %collective-permute-start.39) | collective-permute-done | bytes 32800 | tf_op jit(solution)/shard_map/ppermute | solution.py:461
  7.0 0.0 collective-permute-done.38
  7.0 2.2 %collective-permute-start.41 = (f32[2,16,512]{2,1,0:T(8,128)S(1)}, f32[2,16,512]{2,1,0:T(8,128)S(1)}, u32[]{:S(2)}, u32[]{:S(2)}) collective-permute-start(f32[2,16,512]{2,1,0:T(8,128)S(1)} %maximum_select_fusion.1), channel_id=1, source_target_pairs={{0,8},{4,12},{8,0},{12,4},{16,24},{20,28},{24,16},{28,20},{1,9},{5... | collective-permute-start | bytes 196616 | tf_op jit(solution)/shard_map/ppermute | solution.py:461
  9.2 1.6 %collective-permute-start.40 = (f32[2,3,32,512]{3,2,1,0:T(8,128)S(1)}, f32[2,3,32,512]{3,2,1,0:T(8,128)S(1)}, u32[]{:S(2)}, u32[]{:S(2)}) collective-permute-start(f32[2,3,32,512]{3,2,1,0:T(8,128)S(1)} %fusion.1), channel_id=1, source_target_pairs={{0,4},{4,0},{8,12},{12,8},{16,20},{20,16},{24,28},{28,24},{1,5},{5... | collective-permute-start | bytes 1179656 | tf_op jit(solution)/shard_map/ppermute | solution.py:461
  10.8 0.7 collective-permute-done.41
  11.4 3.1 %collective-permute-start.42 = (f32[4,16,512]{2,1,0:T(8,128)S(1)}, f32[4,16,512]{2,1,0:T(8,128)S(1)}, u32[]{:S(2)}, u32[]{:S(2)}) collective-permute-start(f32[4,16,512]{2,1,0:T(8,128)S(1)} %maximum_select_fusion), channel_id=1, source_target_pairs={{0,16},{4,20},{8,24},{12,28},{16,0},{20,4},{24,8},{28,12},{1,17},{... | collective-permute-start | bytes 393224 | tf_op jit(solution)/shard_map/ppermute | solution.py:461
  14.5 0.1 copy.13
  14.6 0.1 reshape.18.fill_ref
  14.7 1.2 %shard_map.63 = s32[1]{0:T(128)} custom-call(s32[96]{0:T(128)S(1)} %reshape.18.fill_ref), custom_call_target="tpu_custom_call" | custom-call | tf_op jit(solution)/shard_map/pallas_call | solution.py:186
  16.6 0.1 pad_add_fusion
  16.7 2.5 %collective-permute-done.42 = f32[4,16,512]{2,1,0:T(8,128)S(1)} collective-permute-done((f32[4,16,512]{2,1,0:T(8,128)S(1)}, f32[4,16,512]{2,1,0:T(8,128)S(1)}, u32[]{:S(2)}, u32[]{:S(2)}) %collective-permute-start.42) | collective-permute-done | bytes 131104 | tf_op jit(solution)/shard_map/ppermute | solution.py:461
  19.2 0.1 pad_maximum_fusion.7
  19.3 0.0 collective-permute-done.40
  19.3 59.2 %conditional.1 = (f32[384,512]{1,0:T(8,128)}, f32[3072,512]{1,0:T(8,128)}) conditional(s32[]{:T(128)} %bitcast.18, (s32[2]{0:T(128)S(1)}, s32[96]{0:T(128)S(1)}, f32[384,512]{1,0:T(8,128)S(1)}, f32[3,2,32,512]{3,2,1,0:T(8,128)S(1)}, f32[2,3,32,512]{3,2,1,0:T(8,128)S(1)}, /*index=5*/s32[]{:T(128)}, f32[384,512]{1,0:T(8,128)S(1)}, ...), branch_computations={%region_0.1_spmd, %region_1.2_spmd} | conditional | flops 1376297 | bytes 87295320 | solution.py:567
  19.5 0.0 copy-start.9
  19.6 1.6 %collective-permute-start.21 = (f32[8,16,512]{2,1,0:T(8,128)S(1)}, f32[8,16,512]{2,1,0:T(8,128)S(1)}, u32[]{:S(2)}, u32[]{:S(2)}) collective-permute-start(f32[8,16,512]{2,1,0:T(8,128)S(1)} %broadcast_select_fusion.3.refs_0_), channel_id=1, source_target_pairs={{0,2},{1,3},{2,0},{3,1},{4,6},{5,7},{6,4},{7,5},{8,10},{9,11},{10,... | collective-permute-start | bytes 786440 | tf_op jit(solution)/shard_map/cond/branch_1_fun/ppermute | solution.py:461
  21.2 0.9 %branch_1_fun.7.refs_0_ = f32[10,32,256]{2,1,0:T(8,128)S(1)} custom-call(s32[2]{0:T(128)S(1)} %get-tuple-element.66.where_ref, s32[96]{0:T(128)S(1)} %get-tuple-element.67.fill_ref, f32[3,128,512]{2,1,0:T(8,128)S(1)} %bitcast.52, f32[3,2,32,512]{3,2,1,0:T(8,128)S(1)} %get-tuple-element.69.core_ref, f32[2,3,32,512]{3,2,1,0:T(8,128)S(1)} %get-tuple-element.70.side_ref), custom_call_target="tpu_custom_call" | custom-call | tf_op jit(solution)/shard_map/cond/branch_1_fun/pallas_call | solution.py:221
  22.1 3.5 %collective-permute-start.19 = (f32[10,32,256]{2,1,0:T(8,128)S(1)}, f32[10,32,256]{2,1,0:T(8,128)S(1)}, u32[]{:S(2)}, u32[]{:S(2)}) collective-permute-start(f32[10,32,256]{2,1,0:T(8,128)S(1)} %branch_1_fun.7.refs_0_), channel_id=1, source_target_pairs={{0,24},{4,28},{8,0},{12,4},{16,8},{20,12},{24,16},{28,20},{1,25},{... | collective-permute-start | bytes 983048 | tf_op jit(solution)/shard_map/cond/branch_1_fun/ppermute | solution.py:475
  25.6 0.0 collective-permute-start.20
  25.6 0.4 collective-permute-done.21.refs_2_
  26.0 0.1 collective-permute-start.22
  26.2 2.1 %collective-permute-start.25 = (f32[10,32,256]{2,1,0:T(8,128)S(1)}, f32[10,32,256]{2,1,0:T(8,128)S(1)}, u32[]{:S(2)}, u32[]{:S(2)}) collective-permute-start(f32[10,32,256]{2,1,0:T(8,128)S(1)} %branch_1_fun.7.refs_0_), channel_id=1, source_target_pairs={{0,16},{4,20},{8,24},{12,28},{16,0},{20,4},{24,8},{28,12},{1,17},{... | collective-permute-start | bytes 983048 | tf_op jit(solution)/shard_map/cond/branch_1_fun/ppermute | solution.py:475
  28.3 1.5 %collective-permute-start.23 = (f32[10,32,256]{2,1,0:T(8,128)S(1)}, f32[10,32,256]{2,1,0:T(8,128)S(1)}, u32[]{:S(2)}, u32[]{:S(2)}) collective-permute-start(f32[10,32,256]{2,1,0:T(8,128)S(1)} %branch_1_fun.7.refs_0_), channel_id=1, source_target_pairs={{0,4},{4,0},{8,12},{12,8},{16,20},{20,16},{24,28},{28,24},{1,5},{5... | collective-permute-start | bytes 983048 | tf_op jit(solution)/shard_map/cond/branch_1_fun/ppermute | solution.py:461
  29.8 0.0 collective-permute-done.20.refs_1_
  29.8 1.7 %collective-permute-done.19.refs_1_.refs_3_ = f32[10,32,256]{2,1,0:T(8,128)S(1)} collective-permute-done((f32[10,32,256]{2,1,0:T(8,128)S(1)}, f32[10,32,256]{2,1,0:T(8,128)S(1)}, u32[]{:S(2)}, u32[]{:S(2)}) %collective-permute-start.19) | collective-permute-done | bytes 327712 | tf_op jit(solution)/shard_map/cond/branch_1_fun/ppermute | solution.py:475
  31.5 0.0 collective-permute-done.22.refs_3_
  31.5 1.5 %collective-permute-start.24 = (f32[10,32,256]{2,1,0:T(8,128)S(1)}, f32[10,32,256]{2,1,0:T(8,128)S(1)}, u32[]{:S(2)}, u32[]{:S(2)}) collective-permute-start(f32[10,32,256]{2,1,0:T(8,128)S(1)} %collective-permute-done.19.refs_1_.refs_3_), channel_id=1, source_target_pairs={{0,4},{4,0},{8,12},{12,8},{16,20},{20,16},{24,28},{28,24},{1,5},{5... | collective-permute-start | bytes 983048 | tf_op jit(solution)/shard_map/cond/branch_1_fun/ppermute | solution.py:461
  33.0 1.7 %branch_1_fun.9.refs_1_ = f32[2,6,32,256]{3,2,1,0:T(8,128)S(1)} custom-call(s32[2]{0:T(128)S(1)} %get-tuple-element.66.where_ref, s32[96]{0:T(128)S(1)} %get-tuple-element.67.fill_ref, f32[10,32,256]{2,1,0:T(8,128)S(1)} %branch_1_fun.7.refs_0_, f32[10,32,256]{2,1,0:T(8,128)S(1)} %collective-permute-done.19.refs_1_.refs_3_), custom_call_target="tpu_custom_call" | custom-call | tf_op jit(solution)/shard_map/cond/branch_1_fun/pallas_call | solution.py:269
  34.7 6.9 %branch_1_fun.8.w_ref = f32[512,512]{1,0:T(8,128)S(1)} custom-call(s32[2]{0:T(128)S(1)} %get-tuple-element.66.where_ref, f32[8,16,512]{2,1,0:T(8,128)S(1)} %broadcast_select_fusion.3.refs_0_, f32[8,16,512]{2,1,0:T(8,128)S(1)} %collective-permute-done.20.refs_1_, f32[8,16,512]{2,1,0:T(8,128)S(1)} %collective-permute-done.21.refs_2_, ...), custom_call_target="tpu_custom_call" | custom-call | tf_op jit(solution)/shard_map/cond/branch_1_fun/pallas_call | solution.py:106
  41.6 2.5 %collective-permute-done.25.refs_0_.refs_6_ = f32[10,32,256]{2,1,0:T(8,128)S(1)} collective-permute-done((f32[10,32,256]{2,1,0:T(8,128)S(1)}, f32[10,32,256]{2,1,0:T(8,128)S(1)}, u32[]{:S(2)}, u32[]{:S(2)}) %collective-permute-start.25) | collective-permute-done | bytes 327712 | tf_op jit(solution)/shard_map/cond/branch_1_fun/ppermute | solution.py:475
  44.1 1.1 %collective-permute-done.24.refs_4_ = f32[10,32,256]{2,1,0:T(8,128)S(1)} collective-permute-done((f32[10,32,256]{2,1,0:T(8,128)S(1)}, f32[10,32,256]{2,1,0:T(8,128)S(1)}, u32[]{:S(2)}, u32[]{:S(2)}) %collective-permute-start.24) | collective-permute-done | bytes 327712 | tf_op jit(solution)/shard_map/cond/branch_1_fun/ppermute | solution.py:461
  45.2 1.3 %branch_1_fun.10 = f32[2,6,32,256]{3,2,1,0:T(8,128)S(1)} custom-call(s32[2]{0:T(128)S(1)} %get-tuple-element.66.where_ref, s32[96]{0:T(128)S(1)} %get-tuple-element.67.fill_ref, f32[10,32,256]{2,1,0:T(8,128)S(1)} %collective-permute-done.25.refs_0_.refs_6_, f32[2,6,32,256]{3,2,1,0:T(8,128)S(1)} %branch_1_fun.9.refs_1_), custom_call_target="tpu_custom_call" | custom-call | tf_op jit(solution)/shard_map/cond/branch_1_fun/pallas_call | solution.py:269
  46.4 4.2 %collective-permute-start.26 = (f32[2,6,32,256]{3,2,1,0:T(8,128)S(1)}, f32[2,6,32,256]{3,2,1,0:T(8,128)}, u32[]{:S(2)}, u32[]{:S(2)}) collective-permute-start(f32[2,6,32,256]{3,2,1,0:T(8,128)S(1)} %branch_1_fun.10), channel_id=1, source_target_pairs={{0,2},{1,3},{4,6},{5,7},{8,10},{9,11},{12,14},{13,15},{16,18},{17,... | collective-permute-start | bytes 1179656 | tf_op jit(solution)/shard_map/cond/branch_1_fun/ppermute | solution.py:486
  50.6 1.5 %collective-permute-start.28 = (f32[10,32,256]{2,1,0:T(8,128)S(1)}, f32[10,32,256]{2,1,0:T(8,128)S(1)}, u32[]{:S(2)}, u32[]{:S(2)}) collective-permute-start(f32[10,32,256]{2,1,0:T(8,128)S(1)} %collective-permute-done.25.refs_0_.refs_6_), channel_id=1, source_target_pairs={{0,4},{4,0},{8,12},{12,8},{16,20},{20,16},{24,28},{28,24},{1,5},{5... | collective-permute-start | bytes 983048 | tf_op jit(solution)/shard_map/cond/branch_1_fun/ppermute | solution.py:461
  52.1 1.8 %collective-permute-start.27 = (f32[10,32,256]{2,1,0:T(8,128)S(1)}, f32[10,32,256]{2,1,0:T(8,128)S(1)}, u32[]{:S(2)}, u32[]{:S(2)}) collective-permute-start(f32[10,32,256]{2,1,0:T(8,128)S(1)} %branch_1_fun.7.refs_0_), channel_id=1, source_target_pairs={{0,8},{4,12},{8,16},{12,20},{16,24},{20,28},{24,0},{28,4},{1,9},{5... | collective-permute-start | bytes 983048 | tf_op jit(solution)/shard_map/cond/branch_1_fun/ppermute | solution.py:475
  54.0 0.1 collective-permute-start.33
  54.1 4.6 %branch_1_fun.11 = (f32[384,512]{1,0:T(8,128)}, s32[48]{0:T(128)S(1)}, f32[3072,512]{1,0:T(8,128)S(1)}, f32[512,512]{1,0:T(8,128)S(1)}) custom-call(s32[2]{0:T(128)S(1)} %get-tuple-element.66.where_ref, s32[96]{0:T(128)S(1)} %get-tuple-element.67.fill_ref, f32[512,512]{1,0:T(8,128)S(1)} %branch_1_fun.8.w_ref, f32[384,512]{1,0:T(8,128)S(1)} %copy-done.10, ...), custom_call_target="tpu_custom_call" | custom-call | tf_op jit(solution)/shard_map/cond/branch_1_fun/pallas_call | solution.py:320
  58.7 0.0 collective-permute-done.26
  58.7 0.1 broadcast_select_fusion.2
  58.8 0.6 collective-permute-start.31
  59.5 0.2 collective-permute-start.34
  59.8 2.6 %collective-permute-done.27.refs_9_ = f32[10,32,256]{2,1,0:T(8,128)S(1)} collective-permute-done((f32[10,32,256]{2,1,0:T(8,128)S(1)}, f32[10,32,256]{2,1,0:T(8,128)S(1)}, u32[]{:S(2)}, u32[]{:S(2)}) %collective-permute-start.27) | collective-permute-done | bytes 327712 | tf_op jit(solution)/shard_map/cond/branch_1_fun/ppermute | solution.py:475
  62.4 0.0 collective-permute-done.28.refs_7_
  62.4 0.0 collective-permute-start.30
  62.4 0.5 collective-permute-start.29
  62.9 0.1 pad_maximum_fusion.5
  63.0 3.6 %collective-permute-done.31.refs_2_ = f32[6,32,256]{2,1,0:T(8,128)S(1)} collective-permute-done((f32[6,32,256]{2,1,0:T(8,128)S(1)}, f32[6,32,256]{2,1,0:T(8,128)S(1)}, u32[]{:S(2)}, u32[]{:S(2)}) %collective-permute-start.31) | collective-permute-done | bytes 196640 | tf_op jit(solution)/shard_map/cond/branch_1_fun/ppermute | solution.py:461
  66.6 0.0 collective-permute-start.35
  66.6 0.0 collective-permute-done.30.refs_1_
  66.6 0.5 collective-permute-start.32
  67.1 1.9 %collective-permute-done.32.refs_3_ = f32[6,32,256]{2,1,0:T(8,128)S(1)} collective-permute-done((f32[6,32,256]{2,1,0:T(8,128)S(1)}, f32[6,32,256]{2,1,0:T(8,128)S(1)}, u32[]{:S(2)}, u32[]{:S(2)}) %collective-permute-start.32) | collective-permute-done | bytes 196640 | tf_op jit(solution)/shard_map/cond/branch_1_fun/ppermute | solution.py:461
  69.0 0.1 collective-permute-start.36
  69.1 2.3 %branch_1_fun.12.column_ref = f32[512,512]{1,0:T(8,128)S(1)} custom-call(s32[2]{0:T(128)S(1)} %get-tuple-element.66.where_ref, s32[96]{0:T(128)S(1)} %get-tuple-element.67.fill_ref, f32[512,512]{1,0:T(8,128)S(1)} %get-tuple-element.87.inverse_ref, f32[6,32,256]{2,1,0:T(8,128)S(1)} %get-tuple-element.128.refs_0_, ...), custom_call_target="tpu_custom_call" | custom-call | tf_op jit(solution)/shard_map/cond/branch_1_fun/pallas_call | solution.py:365
  71.4 1.8 %collective-permute-done.29.refs_10_ = f32[10,32,256]{2,1,0:T(8,128)S(1)} collective-permute-done((f32[10,32,256]{2,1,0:T(8,128)S(1)}, f32[10,32,256]{2,1,0:T(8,128)S(1)}, u32[]{:S(2)}, u32[]{:S(2)}) %collective-permute-start.29) | collective-permute-done | bytes 327712 | tf_op jit(solution)/shard_map/cond/branch_1_fun/ppermute | solution.py:461
  73.2 0.0 collective-permute-start.37
  73.2 1.6 %collective-permute-done.37.refs_12_ = f32[10,32,256]{2,1,0:T(8,128)S(1)} collective-permute-done((f32[10,32,256]{2,1,0:T(8,128)S(1)}, f32[10,32,256]{2,1,0:T(8,128)S(1)}, u32[]{:S(2)}, u32[]{:S(2)}) %collective-permute-start.37) | collective-permute-done | bytes 327712 | tf_op jit(solution)/shard_map/cond/branch_1_fun/ppermute | solution.py:461
  74.8 3.3 %branch_1_fun.13 = f32[3072,512]{1,0:T(8,128)} custom-call(s32[2]{0:T(128)S(1)} %get-tuple-element.66.where_ref, s32[48]{0:T(128)S(1)} %get-tuple-element.83.slot_ref, f32[512,512]{1,0:T(8,128)S(1)} %branch_1_fun.12.column_ref, f32[3072,512]{1,0:T(8,128)S(1)} %get-tuple-element.91.window_ref, f32[10,32,256]{2,1,0:T(8,128)S(1)} %branch_1_fun.7.refs_0_, ...), custom_call_target="tpu_custom_call" | custom-call | tf_op jit(solution)/shard_map/cond/branch_1_fun/pallas_call | solution.py:444
  78.5 0.0 copy-start.1
  78.5 0.9 %copy-done.1 = f32[64,512]{1,0:T(8,128)S(1)} copy-done((f32[64,512]{1,0:T(8,128)S(1)}, f32[64,512]{1,0:T(8,128)}, u32[]{:S(2)}) %copy-start.1) | copy-done | bytes 131096
  (20 shorter events, 0.2 us)
Async XLA Ops:
  0.6 1.8 %copy-start = (f32[64,512]{1,0:T(8,128)S(1)}, f32[64,512]{1,0:T(8,128)}, u32[]{:S(2)}) copy-start(f32[64,512]{1,0:T(8,128)} %param.8) | copy-start | bytes 393220
  0.7 13.9 %copy-start.11 = (s32[48,2]{0,1:T(2,128)S(1)}, s32[48,2]{0,1:T(2,128)}, u32[]{:S(2)}) copy-start(s32[48,2]{0,1:T(2,128)} %param.9) | copy-start | bytes 1156
  1.9 17.4 %copy-start.6 = (f32[384,512]{1,0:T(8,128)S(1)}, f32[384,512]{1,0:T(8,128)}, u32[]{:S(2)}) copy-start(f32[384,512]{1,0:T(8,128)} %param.7) | copy-start | bytes 2359300
  1.9 5.1 %collective-permute-start.38 = (f32[3,2,32,512]{3,2,1,0:T(8,128)S(1)}, f32[3,2,32,512]{3,2,1,0:T(8,128)S(1)}, u32[]{:S(2)}, u32[]{:S(2)}) collective-permute-start(f32[3,2,32,512]{3,2,1,0:T(8,128)S(1)} %get-tuple-element.130), channel_id=1, source_target_pairs={{0,1},{1,0},{2,3},{3,2},{4,5},{5,4},{6,7},{7,6},{8,9},{9,8},{10,11... | collective-permute-start | bytes 1179656 | tf_op jit(solution)/shard_map/ppermute | solution.py:461
  2.5 4.5 %collective-permute-start.39 = (f32[1,16,512]{2,1,0:T(8,128)S(1)}, f32[1,16,512]{2,1,0:T(8,128)S(1)}, u32[]{:S(2)}, u32[]{:S(2)}) collective-permute-start(f32[1,16,512]{2,1,0:T(8,128)S(1)} %dynamic-slice_bitcast_fusion.6), channel_id=1, source_target_pairs={{0,4},{4,0},{8,12},{12,8},{16,20},{20,16},{24,28},{28,24},{1,5},{5... | collective-permute-start | bytes 98312 | tf_op jit(solution)/shard_map/ppermute | solution.py:461
  7.0 4.4 %collective-permute-start.41 = (f32[2,16,512]{2,1,0:T(8,128)S(1)}, f32[2,16,512]{2,1,0:T(8,128)S(1)}, u32[]{:S(2)}, u32[]{:S(2)}) collective-permute-start(f32[2,16,512]{2,1,0:T(8,128)S(1)} %maximum_select_fusion.1), channel_id=1, source_target_pairs={{0,8},{4,12},{8,0},{12,4},{16,24},{20,28},{24,16},{28,20},{1,9},{5... | collective-permute-start | bytes 196616 | tf_op jit(solution)/shard_map/ppermute | solution.py:461
  9.2 10.1 %collective-permute-start.40 = (f32[2,3,32,512]{3,2,1,0:T(8,128)S(1)}, f32[2,3,32,512]{3,2,1,0:T(8,128)S(1)}, u32[]{:S(2)}, u32[]{:S(2)}) collective-permute-start(f32[2,3,32,512]{3,2,1,0:T(8,128)S(1)} %fusion.1), channel_id=1, source_target_pairs={{0,4},{4,0},{8,12},{12,8},{16,20},{20,16},{24,28},{28,24},{1,5},{5... | collective-permute-start | bytes 1179656 | tf_op jit(solution)/shard_map/ppermute | solution.py:461
  11.4 7.8 %collective-permute-start.42 = (f32[4,16,512]{2,1,0:T(8,128)S(1)}, f32[4,16,512]{2,1,0:T(8,128)S(1)}, u32[]{:S(2)}, u32[]{:S(2)}) collective-permute-start(f32[4,16,512]{2,1,0:T(8,128)S(1)} %maximum_select_fusion), channel_id=1, source_target_pairs={{0,16},{4,20},{8,24},{12,28},{16,0},{20,4},{24,8},{28,12},{1,17},{... | collective-permute-start | bytes 393224 | tf_op jit(solution)/shard_map/ppermute | solution.py:461
  19.5 6.5 %copy-start.9 = (f32[384,512]{1,0:T(8,128)}, f32[384,512]{1,0:T(8,128)S(1)}, u32[]{:S(2)}) copy-start(f32[384,512]{1,0:T(8,128)S(1)} %get-tuple-element.80.panel_ref) | copy-start | bytes 2359300 | tf_op jit(solution)/shard_map/cond
  19.6 6.4 %collective-permute-start.21 = (f32[8,16,512]{2,1,0:T(8,128)S(1)}, f32[8,16,512]{2,1,0:T(8,128)S(1)}, u32[]{:S(2)}, u32[]{:S(2)}) collective-permute-start(f32[8,16,512]{2,1,0:T(8,128)S(1)} %broadcast_select_fusion.3.refs_0_), channel_id=1, source_target_pairs={{0,2},{1,3},{2,0},{3,1},{4,6},{5,7},{6,4},{7,5},{8,10},{9,11},{10,... | collective-permute-start | bytes 786440 | tf_op jit(solution)/shard_map/cond/branch_1_fun/ppermute | solution.py:461
  22.1 9.4 %collective-permute-start.19 = (f32[10,32,256]{2,1,0:T(8,128)S(1)}, f32[10,32,256]{2,1,0:T(8,128)S(1)}, u32[]{:S(2)}, u32[]{:S(2)}) collective-permute-start(f32[10,32,256]{2,1,0:T(8,128)S(1)} %branch_1_fun.7.refs_0_), channel_id=1, source_target_pairs={{0,24},{4,28},{8,0},{12,4},{16,8},{20,12},{24,16},{28,20},{1,25},{... | collective-permute-start | bytes 983048 | tf_op jit(solution)/shard_map/cond/branch_1_fun/ppermute | solution.py:475
  25.6 4.2 %collective-permute-start.20 = (f32[8,16,512]{2,1,0:T(8,128)S(1)}, f32[8,16,512]{2,1,0:T(8,128)S(1)}, u32[]{:S(2)}, u32[]{:S(2)}) collective-permute-start(f32[8,16,512]{2,1,0:T(8,128)S(1)} %broadcast_select_fusion.3.refs_0_), channel_id=1, source_target_pairs={{0,1},{1,0},{2,3},{3,2},{4,5},{5,4},{6,7},{7,6},{8,9},{9,8},{10,11... | collective-permute-start | bytes 786440 | tf_op jit(solution)/shard_map/cond/branch_1_fun/ppermute | solution.py:461
  26.0 5.5 %collective-permute-start.22 = (f32[8,16,512]{2,1,0:T(8,128)S(1)}, f32[8,16,512]{2,1,0:T(8,128)S(1)}, u32[]{:S(2)}, u32[]{:S(2)}) collective-permute-start(f32[8,16,512]{2,1,0:T(8,128)S(1)} %collective-permute-done.21.refs_2_), channel_id=1, source_target_pairs={{0,1},{1,0},{2,3},{3,2},{4,5},{5,4},{6,7},{7,6},{8,9},{9,8},{10,11... | collective-permute-start | bytes 786440 | tf_op jit(solution)/shard_map/cond/branch_1_fun/ppermute | solution.py:461
  26.2 17.9 %collective-permute-start.25 = (f32[10,32,256]{2,1,0:T(8,128)S(1)}, f32[10,32,256]{2,1,0:T(8,128)S(1)}, u32[]{:S(2)}, u32[]{:S(2)}) collective-permute-start(f32[10,32,256]{2,1,0:T(8,128)S(1)} %branch_1_fun.7.refs_0_), channel_id=1, source_target_pairs={{0,16},{4,20},{8,24},{12,28},{16,0},{20,4},{24,8},{28,12},{1,17},{... | collective-permute-start | bytes 983048 | tf_op jit(solution)/shard_map/cond/branch_1_fun/ppermute | solution.py:475
  28.3 15.8 %collective-permute-start.23 = (f32[10,32,256]{2,1,0:T(8,128)S(1)}, f32[10,32,256]{2,1,0:T(8,128)S(1)}, u32[]{:S(2)}, u32[]{:S(2)}) collective-permute-start(f32[10,32,256]{2,1,0:T(8,128)S(1)} %branch_1_fun.7.refs_0_), channel_id=1, source_target_pairs={{0,4},{4,0},{8,12},{12,8},{16,20},{20,16},{24,28},{28,24},{1,5},{5... | collective-permute-start | bytes 983048 | tf_op jit(solution)/shard_map/cond/branch_1_fun/ppermute | solution.py:461
  31.5 13.7 %collective-permute-start.24 = (f32[10,32,256]{2,1,0:T(8,128)S(1)}, f32[10,32,256]{2,1,0:T(8,128)S(1)}, u32[]{:S(2)}, u32[]{:S(2)}) collective-permute-start(f32[10,32,256]{2,1,0:T(8,128)S(1)} %collective-permute-done.19.refs_1_.refs_3_), channel_id=1, source_target_pairs={{0,4},{4,0},{8,12},{12,8},{16,20},{20,16},{24,28},{28,24},{1,5},{5... | collective-permute-start | bytes 983048 | tf_op jit(solution)/shard_map/cond/branch_1_fun/ppermute | solution.py:461
  46.4 12.3 %collective-permute-start.26 = (f32[2,6,32,256]{3,2,1,0:T(8,128)S(1)}, f32[2,6,32,256]{3,2,1,0:T(8,128)}, u32[]{:S(2)}, u32[]{:S(2)}) collective-permute-start(f32[2,6,32,256]{3,2,1,0:T(8,128)S(1)} %branch_1_fun.10), channel_id=1, source_target_pairs={{0,2},{1,3},{4,6},{5,7},{8,10},{9,11},{12,14},{13,15},{16,18},{17,... | collective-permute-start | bytes 1179656 | tf_op jit(solution)/shard_map/cond/branch_1_fun/ppermute | solution.py:486
  50.6 3.4 %copy-start.10 = (f32[384,512]{1,0:T(8,128)S(1)}, f32[384,512]{1,0:T(8,128)}, u32[]{:S(2)}) copy-start(f32[384,512]{1,0:T(8,128)} %copy-done.9) | copy-start | bytes 2359300 | tf_op jit(solution)/shard_map/cond
  50.6 11.8 %collective-permute-start.28 = (f32[10,32,256]{2,1,0:T(8,128)S(1)}, f32[10,32,256]{2,1,0:T(8,128)S(1)}, u32[]{:S(2)}, u32[]{:S(2)}) collective-permute-start(f32[10,32,256]{2,1,0:T(8,128)S(1)} %collective-permute-done.25.refs_0_.refs_6_), channel_id=1, source_target_pairs={{0,4},{4,0},{8,12},{12,8},{16,20},{20,16},{24,28},{28,24},{1,5},{5... | collective-permute-start | bytes 983048 | tf_op jit(solution)/shard_map/cond/branch_1_fun/ppermute | solution.py:461
  52.1 10.3 %collective-permute-start.27 = (f32[10,32,256]{2,1,0:T(8,128)S(1)}, f32[10,32,256]{2,1,0:T(8,128)S(1)}, u32[]{:S(2)}, u32[]{:S(2)}) collective-permute-start(f32[10,32,256]{2,1,0:T(8,128)S(1)} %branch_1_fun.7.refs_0_), channel_id=1, source_target_pairs={{0,8},{4,12},{8,16},{12,20},{16,24},{20,28},{24,0},{28,4},{1,9},{5... | collective-permute-start | bytes 983048 | tf_op jit(solution)/shard_map/cond/branch_1_fun/ppermute | solution.py:475
  54.0 19.3 %collective-permute-start.33 = (f32[2,10,32,256]{3,2,1,0:T(8,128)S(1)}, f32[2,10,32,256]{3,2,1,0:T(8,128)S(1)}, u32[]{:S(2)}, u32[]{:S(2)}) collective-permute-start(f32[2,10,32,256]{3,2,1,0:T(8,128)S(1)} %pad_maximum_fusion.3), channel_id=1, source_target_pairs={{0,1},{1,0},{2,3},{3,2},{4,5},{5,4},{6,7},{7,6},{8,9},{9,8},{10,11... | collective-permute-start | bytes 1966088 | tf_op jit(solution)/shard_map/cond/branch_1_fun/ppermute | solution.py:461
  58.8 7.8 %collective-permute-start.31 = (f32[6,32,256]{2,1,0:T(8,128)S(1)}, f32[6,32,256]{2,1,0:T(8,128)S(1)}, u32[]{:S(2)}, u32[]{:S(2)}) collective-permute-start(f32[6,32,256]{2,1,0:T(8,128)S(1)} %get-tuple-element.127), channel_id=1, source_target_pairs={{0,4},{4,0},{8,12},{12,8},{16,20},{20,16},{24,28},{28,24},{1,5},{5... | collective-permute-start | bytes 589832 | tf_op jit(solution)/shard_map/cond/branch_1_fun/ppermute | solution.py:461
  59.5 13.7 %collective-permute-start.34 = (f32[2,10,32,256]{3,2,1,0:T(8,128)S(1)}, f32[2,10,32,256]{3,2,1,0:T(8,128)S(1)}, u32[]{:S(2)}, u32[]{:S(2)}) collective-permute-start(f32[2,10,32,256]{3,2,1,0:T(8,128)S(1)} %pad_maximum_fusion.4), channel_id=1, source_target_pairs={{0,1},{1,0},{2,3},{3,2},{4,5},{5,4},{6,7},{7,6},{8,9},{9,8},{10,11... | collective-permute-start | bytes 1966088 | tf_op jit(solution)/shard_map/cond/branch_1_fun/ppermute | solution.py:461
  62.4 4.2 %collective-permute-start.30 = (f32[6,32,256]{2,1,0:T(8,128)S(1)}, f32[6,32,256]{2,1,0:T(8,128)S(1)}, u32[]{:S(2)}, u32[]{:S(2)}) collective-permute-start(f32[6,32,256]{2,1,0:T(8,128)S(1)} %get-tuple-element.128.refs_0_), channel_id=1, source_target_pairs={{0,1},{1,0},{2,3},{3,2},{4,5},{5,4},{6,7},{7,6},{8,9},{9,8},{10,11... | collective-permute-start | bytes 589832 | tf_op jit(solution)/shard_map/cond/branch_1_fun/ppermute | solution.py:461
  62.4 10.8 %collective-permute-start.29 = (f32[10,32,256]{2,1,0:T(8,128)S(1)}, f32[10,32,256]{2,1,0:T(8,128)S(1)}, u32[]{:S(2)}, u32[]{:S(2)}) collective-permute-start(f32[10,32,256]{2,1,0:T(8,128)S(1)} %collective-permute-done.27.refs_9_), channel_id=1, source_target_pairs={{0,4},{4,0},{8,12},{12,8},{16,20},{20,16},{24,28},{28,24},{1,5},{5... | collective-permute-start | bytes 983048 | tf_op jit(solution)/shard_map/cond/branch_1_fun/ppermute | solution.py:461
  66.6 6.6 %collective-permute-start.35 = (f32[2,10,32,256]{3,2,1,0:T(8,128)S(1)}, f32[2,10,32,256]{3,2,1,0:T(8,128)S(1)}, u32[]{:S(2)}, u32[]{:S(2)}) collective-permute-start(f32[2,10,32,256]{3,2,1,0:T(8,128)S(1)} %pad_maximum_fusion.5), channel_id=1, source_target_pairs={{0,1},{1,0},{2,3},{3,2},{4,5},{5,4},{6,7},{7,6},{8,9},{9,8},{10,11... | collective-permute-start | bytes 1966088 | tf_op jit(solution)/shard_map/cond/branch_1_fun/ppermute | solution.py:461
  66.6 2.4 %collective-permute-start.32 = (f32[6,32,256]{2,1,0:T(8,128)S(1)}, f32[6,32,256]{2,1,0:T(8,128)S(1)}, u32[]{:S(2)}, u32[]{:S(2)}) collective-permute-start(f32[6,32,256]{2,1,0:T(8,128)S(1)} %collective-permute-done.31.refs_2_), channel_id=1, source_target_pairs={{0,1},{1,0},{2,3},{3,2},{4,5},{5,4},{6,7},{7,6},{8,9},{9,8},{10,11... | collective-permute-start | bytes 589832 | tf_op jit(solution)/shard_map/cond/branch_1_fun/ppermute | solution.py:461
  69.0 4.3 %collective-permute-start.36 = (f32[10,32,256]{2,1,0:T(8,128)S(1)}, f32[10,32,256]{2,1,0:T(8,128)S(1)}, u32[]{:S(2)}, u32[]{:S(2)}) collective-permute-start(f32[10,32,256]{2,1,0:T(8,128)S(1)} %collective-permute-done.27.refs_9_), channel_id=1, source_target_pairs={{0,1},{1,0},{2,3},{3,2},{4,5},{5,4},{6,7},{7,6},{8,9},{9,8},{10,11... | collective-permute-start | bytes 983048 | tf_op jit(solution)/shard_map/cond/branch_1_fun/ppermute | solution.py:461
  73.2 1.6 %collective-permute-start.37 = (f32[10,32,256]{2,1,0:T(8,128)S(1)}, f32[10,32,256]{2,1,0:T(8,128)S(1)}, u32[]{:S(2)}, u32[]{:S(2)}) collective-permute-start(f32[10,32,256]{2,1,0:T(8,128)S(1)} %collective-permute-done.29.refs_10_), channel_id=1, source_target_pairs={{0,1},{1,0},{2,3},{3,2},{4,5},{5,4},{6,7},{7,6},{8,9},{9,8},{10,11... | collective-permute-start | bytes 983048 | tf_op jit(solution)/shard_map/cond/branch_1_fun/ppermute | solution.py:461
  78.5 0.9 %copy-start.1 = (f32[64,512]{1,0:T(8,128)S(1)}, f32[64,512]{1,0:T(8,128)}, u32[]{:S(2)}) copy-start(f32[64,512]{1,0:T(8,128)} %param.8) | copy-start | bytes 393220
where the time goes:
time: 79.8 us; the launch traced here: 79.4 us
  starting transfers between devices  29.9 us (37%)
  waiting for transfers between devices  22.3 us (28%)
  Pallas kernels  22.2 us (28%)
  local copies, waits for them, and re-layouts  2.41 us (3%)
  between operations  1.41 us (2%)
    ppermute x20, starting transfers between devices, swap(): return lax.ppermute(value, axis, [(i, i ^ step) for i in range(size)])  18.3 us
    ppermute x20, waiting for transfers between devices, swap(): return lax.ppermute(value, axis, [(i, i ^ step) for i in range(size)])  15.4 us
    ppermute x3, starting transfers between devices, bring(): return lax.ppermute(value, 'col', pairs)  7.48 us
    pallas_call x1, Pallas kernels, inverse_factor(): pl.pallas_call(inverse_factor_kernel, out_shape=jax.ShapeDtypeStruct((n,...  6.89 us
    ppermute x3, waiting for transfers between devices, bring(): return lax.ppermute(value, 'col', pairs)  6.82 us
    pallas_call x1, Pallas kernels, own_factor(): pl.pallas_call(functools.partial(own_factor_kernel, sizes), out_shape=(pl...  4.65 us
    ppermute x1, starting transfers between devices, spread_column(): other = lax.ppermute(value, ('col', 'row'), pairs)  4.18 us
    pallas_call x1, Pallas kernels, update(): pl.pallas_call(functools.partial(update_kernel, sizes, [len(group) for gr...  3.34 us
  transfers between devices with their start and end apart: 24, of which 12 were waited for; matrix products, arithmetic and copies ran while one was open for 1% of the time, Pallas kernels for 22%

commit v1 on v0

--- a/solution.py
+++ b/solution.py
@@ -526,7 +526,7 @@
         parts = [pivot] + ([swap(pivot, "row", 2)] if split == 4 else [])
         parts = [part for value in parts for part in (value, swap(value, "row", 1))]
         near = first[0]
-        lists[near], *parts = lax.optimization_barrier((lists[near], *parts))
+        lists[near], sides[0], *parts = lax.optimization_barrier((lists[near], sides[0], *parts))
         sides[near] = swap(lists[near], "col", 1)
         w = inverse_factor(where, parts)
         soon, rest = [0, near], [s for s in sizes.needed if s not in (0, near)]

time: 79.8 us -> 80.6 us (1.010)
  starting transfers between devices: 29.9 us -> 27.5 us
  waiting for transfers between devices: 22.3 us -> 24.1 us
  Pallas kernels: 22.2 us -> 23.5 us
    ppermute x3, waiting for transfers between devices: 6.82 us -> 10.8 us  [bring(): return lax.ppermute(value, 'col', pairs)]
    ppermute x20, waiting for transfers between devices: 15.4 us -> 13.2 us  [swap(): return lax.ppermute(value, axis, [(i, i ^ step) for i in range(size)])]
    ppermute x3, starting transfers between devices: 7.48 us -> 5.35 us  [bring(): return lax.ppermute(value, 'col', pairs)]
    pallas_call x1, Pallas kernels: 3.34 us -> 4.56 us  [update(): pl.pallas_call(functools.partial(update_kernel, sizes, [len(group) for gr...]
    ppermute x1, starting transfers between devices: 4.18 us -> 3.17 us  [spread_column(): other = lax.ppermute(value, ('col', 'row'), pairs)]
where the time goes in v1:
time: 80.6 us; the launch traced here: 80 us
  starting transfers between devices  27.5 us (34%)
  waiting for transfers between devices  24.1 us (30%)
  Pallas kernels  23.5 us (29%)
  local copies, waits for them, and re-layouts  2.41 us (3%)
  between operations  1.41 us (2%)
    ppermute x20, starting transfers between devices, swap(): return lax.ppermute(value, axis, [(i, i ^ step) for i in range(size)])  19 us
    ppermute x20, waiting for transfers between devices, swap(): return lax.ppermute(value, axis, [(i, i ^ step) for i in range(size)])  13.2 us
    ppermute x3, waiting for transfers between devices, bring(): return lax.ppermute(value, 'col', pairs)  10.8 us
    pallas_call x1, Pallas kernels, inverse_factor(): pl.pallas_call(inverse_factor_kernel, out_shape=jax.ShapeDtypeStruct((n,...  6.89 us
    ppermute x3, starting transfers between devices, bring(): return lax.ppermute(value, 'col', pairs)  5.35 us
    pallas_call x1, Pallas kernels, own_factor(): pl.pallas_call(functools.partial(own_factor_kernel, sizes), out_shape=(pl...  4.64 us
    pallas_call x1, Pallas kernels, update(): pl.pallas_call(functools.partial(update_kernel, sizes, [len(group) for gr...  4.56 us
    ppermute x1, starting transfers between devices, spread_column(): other = lax.ppermute(value, ('col', 'row'), pairs)  3.17 us
  transfers between devices with their start and end apart: 24, of which 12 were waited for; matrix products, arithmetic and copies ran while one was open for 1% of the time, Pallas kernels for 22%

profile of v1, /device:TPU:0, one launch (start us, length us, event | category | flops | bytes accessed | tf_op | source)
XLA Modules:
  0.0 80.0 jit_solution(6543593216125514592)
XLA Ops:
  0.6 0.0 copy-start
  0.7 1.2 %dynamic-slice_bitcast_fusion.4 = (f32[1,3,2,32,512]{4,3,2,1,0:T(8,128)S(1)}, f32[3,2,32,512]{3,2,1,0:T(8,128)S(1)}) fusion(f32[3,2,2,32,512]{4,3,2,1,0:T(8,128)} %bitcast.50, s32[]{:T(128)S(6)} %select_n.102, s32[]{:T(128)S(6)} %select_n.97), kind=kLoop, calls=%fused_computation.18 | loop fusion | bytes 1572872 | tf_op jit(solution)/shard_map/stack | solution.py:512
  1.9 0.0 copy-start.6
  1.9 0.5 collective-permute-start.38
  2.5 2.6 %collective-permute-start.39 = (f32[1,16,512]{2,1,0:T(8,128)S(1)}, f32[1,16,512]{2,1,0:T(8,128)S(1)}, u32[]{:S(2)}, u32[]{:S(2)}) collective-permute-start(f32[1,16,512]{2,1,0:T(8,128)S(1)} %dynamic-slice_bitcast_fusion.6), channel_id=1, source_target_pairs={{0,4},{4,0},{8,12},{12,8},{16,20},{20,16},{24,28},{28,24},{1,5},{5... | collective-permute-start | bytes 98312 | tf_op jit(solution)/shard_map/ppermute | solution.py:461
  5.1 1.9 %collective-permute-done.39 = f32[1,16,512]{2,1,0:T(8,128)S(1)} collective-permute-done((f32[1,16,512]{2,1,0:T(8,128)S(1)}, f32[1,16,512]{2,1,0:T(8,128)S(1)}, u32[]{:S(2)}, u32[]{:S(2)}) %collective-permute-start.39) | collective-permute-done | bytes 32800 | tf_op jit(solution)/shard_map/ppermute | solution.py:461
  7.0 0.0 collective-permute-done.38
  7.0 2.2 %collective-permute-start.41 = (f32[2,16,512]{2,1,0:T(8,128)S(1)}, f32[2,16,512]{2,1,0:T(8,128)S(1)}, u32[]{:S(2)}, u32[]{:S(2)}) collective-permute-start(f32[2,16,512]{2,1,0:T(8,128)S(1)} %maximum_select_fusion.1), channel_id=1, source_target_pairs={{0,8},{4,12},{8,0},{12,4},{16,24},{20,28},{24,16},{28,20},{1,9},{5... | collective-permute-start | bytes 196616 | tf_op jit(solution)/shard_map/ppermute | solution.py:461
  9.2 1.6 %collective-permute-start.40 = (f32[2,3,32,512]{3,2,1,0:T(8,128)S(1)}, f32[2,3,32,512]{3,2,1,0:T(8,128)S(1)}, u32[]{:S(2)}, u32[]{:S(2)}) collective-permute-start(f32[2,3,32,512]{3,2,1,0:T(8,128)S(1)} %fusion.1), channel_id=1, source_target_pairs={{0,4},{4,0},{8,12},{12,8},{16,20},{20,16},{24,28},{28,24},{1,5},{5... | collective-permute-start | bytes 1179656 | tf_op jit(solution)/shard_map/ppermute | solution.py:461
  10.8 0.7 collective-permute-done.41
  11.4 3.1 %collective-permute-start.42 = (f32[4,16,512]{2,1,0:T(8,128)S(1)}, f32[4,16,512]{2,1,0:T(8,128)S(1)}, u32[]{:S(2)}, u32[]{:S(2)}) collective-permute-start(f32[4,16,512]{2,1,0:T(8,128)S(1)} %maximum_select_fusion), channel_id=1, source_target_pairs={{0,16},{4,20},{8,24},{12,28},{16,0},{20,4},{24,8},{28,12},{1,17},{... | collective-permute-start | bytes 393224 | tf_op jit(solution)/shard_map/ppermute | solution.py:461
  14.5 0.1 copy.13
  14.6 0.1 reshape.18.fill_ref
  14.7 1.2 %shard_map.63 = s32[1]{0:T(128)} custom-call(s32[96]{0:T(128)S(1)} %reshape.18.fill_ref), custom_call_target="tpu_custom_call" | custom-call | tf_op jit(solution)/shard_map/pallas_call | solution.py:186
  16.6 0.1 pad_add_fusion
  16.7 2.5 %collective-permute-done.42 = f32[4,16,512]{2,1,0:T(8,128)S(1)} collective-permute-done((f32[4,16,512]{2,1,0:T(8,128)S(1)}, f32[4,16,512]{2,1,0:T(8,128)S(1)}, u32[]{:S(2)}, u32[]{:S(2)}) %collective-permute-start.42) | collective-permute-done | bytes 131104 | tf_op jit(solution)/shard_map/ppermute | solution.py:461
  19.2 0.1 pad_maximum_fusion.7
  19.3 0.0 collective-permute-done.40
  19.3 59.8 %conditional.1 = (f32[384,512]{1,0:T(8,128)}, f32[3072,512]{1,0:T(8,128)}) conditional(s32[]{:T(128)} %bitcast.18, (s32[2]{0:T(128)S(1)}, s32[96]{0:T(128)S(1)}, f32[384,512]{1,0:T(8,128)S(1)}, f32[3,2,32,512]{3,2,1,0:T(8,128)S(1)}, f32[2,3,32,512]{3,2,1,0:T(8,128)S(1)}, /*index=5*/s32[]{:T(128)}, f32[384,512]{1,0:T(8,128)S(1)}, ...), branch_computations={%region_0.1_spmd, %region_1.2_spmd} | conditional | flops 1376297 | bytes 87295320 | solution.py:567
  19.5 0.0 copy-start.9
  19.6 1.6 %collective-permute-start.22 = (f32[8,16,512]{2,1,0:T(8,128)S(1)}, f32[8,16,512]{2,1,0:T(8,128)S(1)}, u32[]{:S(2)}, u32[]{:S(2)}) collective-permute-start(f32[8,16,512]{2,1,0:T(8,128)S(1)} %broadcast_select_fusion.3.refs_0_), channel_id=1, source_target_pairs={{0,2},{1,3},{2,0},{3,1},{4,6},{5,7},{6,4},{7,5},{8,10},{9,11},{10,... | collective-permute-start | bytes 786440 | tf_op jit(solution)/shard_map/cond/branch_1_fun/ppermute | solution.py:461
  21.2 0.9 %branch_1_fun.7.refs_0_ = f32[10,32,256]{2,1,0:T(8,128)S(1)} custom-call(s32[2]{0:T(128)S(1)} %get-tuple-element.67.where_ref, s32[96]{0:T(128)S(1)} %get-tuple-element.68.fill_ref, f32[3,128,512]{2,1,0:T(8,128)S(1)} %bitcast.52, f32[3,2,32,512]{3,2,1,0:T(8,128)S(1)} %get-tuple-element.70.core_ref, f32[2,3,32,512]{3,2,1,0:T(8,128)S(1)} %get-tuple-element.71.side_ref), custom_call_target="tpu_custom_call" | custom-call | tf_op jit(solution)/shard_map/cond/branch_1_fun/pallas_call | solution.py:221
  22.1 1.6 %collective-permute-start.20 = (f32[10,32,256]{2,1,0:T(8,128)S(1)}, f32[10,32,256]{2,1,0:T(8,128)S(1)}, u32[]{:S(2)}, u32[]{:S(2)}) collective-permute-start(f32[10,32,256]{2,1,0:T(8,128)S(1)} %branch_1_fun.7.refs_0_), channel_id=1, source_target_pairs={{0,4},{4,0},{8,12},{12,8},{16,20},{20,16},{24,28},{28,24},{1,5},{5... | collective-permute-start | bytes 983048 | tf_op jit(solution)/shard_map/cond/branch_1_fun/ppermute | solution.py:461
  23.7 3.5 %collective-permute-start.19 = (f32[10,32,256]{2,1,0:T(8,128)S(1)}, f32[10,32,256]{2,1,0:T(8,128)S(1)}, u32[]{:S(2)}, u32[]{:S(2)}) collective-permute-start(f32[10,32,256]{2,1,0:T(8,128)S(1)} %branch_1_fun.7.refs_0_), channel_id=1, source_target_pairs={{0,24},{4,28},{8,0},{12,4},{16,8},{20,12},{24,16},{28,20},{1,25},{... | collective-permute-start | bytes 983048 | tf_op jit(solution)/shard_map/cond/branch_1_fun/ppermute | solution.py:475
  27.1 0.0 collective-permute-start.21
  27.2 0.5 collective-permute-start.23
  27.7 0.6 collective-permute-start.25
  28.3 0.4 collective-permute-done.21.refs_1_
  28.7 0.6 collective-permute-done.20.refs_1_
  29.3 5.4 %collective-permute-done.19.refs_1_.refs_3_ = f32[10,32,256]{2,1,0:T(8,128)S(1)} collective-permute-done((f32[10,32,256]{2,1,0:T(8,128)S(1)}, f32[10,32,256]{2,1,0:T(8,128)S(1)}, u32[]{:S(2)}, u32[]{:S(2)}) %collective-permute-start.19) | collective-permute-done | bytes 327712 | tf_op jit(solution)/shard_map/cond/branch_1_fun/ppermute | solution.py:475
  34.6 0.0 collective-permute-done.23.refs_3_
  34.7 1.7 %branch_1_fun.9.refs_1_ = f32[2,6,32,256]{3,2,1,0:T(8,128)S(1)} custom-call(s32[2]{0:T(128)S(1)} %get-tuple-element.67.where_ref, s32[96]{0:T(128)S(1)} %get-tuple-element.68.fill_ref, f32[10,32,256]{2,1,0:T(8,128)S(1)} %branch_1_fun.7.refs_0_, f32[10,32,256]{2,1,0:T(8,128)S(1)} %collective-permute-done.19.refs_1_.refs_3_), custom_call_target="tpu_custom_call" | custom-call | tf_op jit(solution)/shard_map/cond/branch_1_fun/pallas_call | solution.py:269
  36.3 6.9 %branch_1_fun.8.w_ref = f32[512,512]{1,0:T(8,128)S(1)} custom-call(s32[2]{0:T(128)S(1)} %get-tuple-element.67.where_ref, f32[8,16,512]{2,1,0:T(8,128)S(1)} %broadcast_select_fusion.3.refs_0_, f32[8,16,512]{2,1,0:T(8,128)S(1)} %collective-permute-done.21.refs_1_, f32[8,16,512]{2,1,0:T(8,128)S(1)} %collective-permute-done.22.refs_2_, ...), custom_call_target="tpu_custom_call" | custom-call | tf_op jit(solution)/shard_map/cond/branch_1_fun/pallas_call | solution.py:106
  43.2 2.1 %collective-permute-done.25.refs_0_.refs_6_ = f32[10,32,256]{2,1,0:T(8,128)S(1)} collective-permute-done((f32[10,32,256]{2,1,0:T(8,128)S(1)}, f32[10,32,256]{2,1,0:T(8,128)S(1)}, u32[]{:S(2)}, u32[]{:S(2)}) %collective-permute-start.25) | collective-permute-done | bytes 327712 | tf_op jit(solution)/shard_map/cond/branch_1_fun/ppermute | solution.py:475
  45.3 0.0 collective-permute-done.24.refs_4_
  45.3 1.3 %branch_1_fun.10 = f32[2,6,32,256]{3,2,1,0:T(8,128)S(1)} custom-call(s32[2]{0:T(128)S(1)} %get-tuple-element.67.where_ref, s32[96]{0:T(128)S(1)} %get-tuple-element.68.fill_ref, f32[10,32,256]{2,1,0:T(8,128)S(1)} %collective-permute-done.25.refs_0_.refs_6_, f32[2,6,32,256]{3,2,1,0:T(8,128)S(1)} %branch_1_fun.9.refs_1_), custom_call_target="tpu_custom_call" | custom-call | tf_op jit(solution)/shard_map/cond/branch_1_fun/pallas_call | solution.py:269
  46.6 3.2 %collective-permute-start.26 = (f32[2,6,32,256]{3,2,1,0:T(8,128)S(1)}, f32[2,6,32,256]{3,2,1,0:T(8,128)}, u32[]{:S(2)}, u32[]{:S(2)}) collective-permute-start(f32[2,6,32,256]{3,2,1,0:T(8,128)S(1)} %branch_1_fun.10), channel_id=1, source_target_pairs={{0,2},{1,3},{4,6},{5,7},{8,10},{9,11},{12,14},{13,15},{16,18},{17,... | collective-permute-start | bytes 1179656 | tf_op jit(solution)/shard_map/cond/branch_1_fun/ppermute | solution.py:486
  49.7 1.3 %collective-permute-start.28 = (f32[10,32,256]{2,1,0:T(8,128)S(1)}, f32[10,32,256]{2,1,0:T(8,128)S(1)}, u32[]{:S(2)}, u32[]{:S(2)}) collective-permute-start(f32[10,32,256]{2,1,0:T(8,128)S(1)} %collective-permute-done.25.refs_0_.refs_6_), channel_id=1, source_target_pairs={{0,4},{4,0},{8,12},{12,8},{16,20},{20,16},{24,28},{28,24},{1,5},{5... | collective-permute-start | bytes 983048 | tf_op jit(solution)/shard_map/cond/branch_1_fun/ppermute | solution.py:461
  51.0 1.2 %collective-permute-start.27 = (f32[10,32,256]{2,1,0:T(8,128)S(1)}, f32[10,32,256]{2,1,0:T(8,128)S(1)}, u32[]{:S(2)}, u32[]{:S(2)}) collective-permute-start(f32[10,32,256]{2,1,0:T(8,128)S(1)} %branch_1_fun.7.refs_0_), channel_id=1, source_target_pairs={{0,8},{4,12},{8,16},{12,20},{16,24},{20,28},{24,0},{28,4},{1,9},{5... | collective-permute-start | bytes 983048 | tf_op jit(solution)/shard_map/cond/branch_1_fun/ppermute | solution.py:475
  52.3 0.1 collective-permute-start.33
  52.4 4.6 %branch_1_fun.11 = (f32[384,512]{1,0:T(8,128)}, s32[48]{0:T(128)S(1)}, f32[3072,512]{1,0:T(8,128)S(1)}, f32[512,512]{1,0:T(8,128)S(1)}) custom-call(s32[2]{0:T(128)S(1)} %get-tuple-element.67.where_ref, s32[96]{0:T(128)S(1)} %get-tuple-element.68.fill_ref, f32[512,512]{1,0:T(8,128)S(1)} %branch_1_fun.8.w_ref, f32[384,512]{1,0:T(8,128)S(1)} %copy-done.10, ...), custom_call_target="tpu_custom_call" | custom-call | tf_op jit(solution)/shard_map/cond/branch_1_fun/pallas_call | solution.py:320
  57.1 0.1 broadcast_select_fusion.2
  57.2 1.6 %collective-permute-start.31 = (f32[6,32,256]{2,1,0:T(8,128)S(1)}, f32[6,32,256]{2,1,0:T(8,128)S(1)}, u32[]{:S(2)}, u32[]{:S(2)}) collective-permute-start(f32[6,32,256]{2,1,0:T(8,128)S(1)} %get-tuple-element.129), channel_id=1, source_target_pairs={{0,4},{4,0},{8,12},{12,8},{16,20},{20,16},{24,28},{28,24},{1,5},{5... | collective-permute-start | bytes 589832 | tf_op jit(solution)/shard_map/cond/branch_1_fun/ppermute | solution.py:461
  58.8 0.3 collective-permute-start.34
  59.1 3.4 %collective-permute-done.27.refs_9_ = f32[10,32,256]{2,1,0:T(8,128)S(1)} collective-permute-done((f32[10,32,256]{2,1,0:T(8,128)S(1)}, f32[10,32,256]{2,1,0:T(8,128)S(1)}, u32[]{:S(2)}, u32[]{:S(2)}) %collective-permute-start.27) | collective-permute-done | bytes 327712 | tf_op jit(solution)/shard_map/cond/branch_1_fun/ppermute | solution.py:475
  62.4 0.0 collective-permute-start.30
  62.4 1.5 %collective-permute-start.29 = (f32[10,32,256]{2,1,0:T(8,128)S(1)}, f32[10,32,256]{2,1,0:T(8,128)S(1)}, u32[]{:S(2)}, u32[]{:S(2)}) collective-permute-start(f32[10,32,256]{2,1,0:T(8,128)S(1)} %collective-permute-done.27.refs_9_), channel_id=1, source_target_pairs={{0,4},{4,0},{8,12},{12,8},{16,20},{20,16},{24,28},{28,24},{1,5},{5... | collective-permute-start | bytes 983048 | tf_op jit(solution)/shard_map/cond/branch_1_fun/ppermute | solution.py:461
  63.9 0.1 pad_maximum_fusion.5
  64.0 0.5 collective-permute-done.31.refs_2_
  64.5 0.0 collective-permute-start.35
  64.5 0.0 collective-permute-done.30.refs_1_
  64.5 0.5 collective-permute-start.32
  65.1 1.9 %collective-permute-done.32.refs_3_ = f32[6,32,256]{2,1,0:T(8,128)S(1)} collective-permute-done((f32[6,32,256]{2,1,0:T(8,128)S(1)}, f32[6,32,256]{2,1,0:T(8,128)S(1)}, u32[]{:S(2)}, u32[]{:S(2)}) %collective-permute-start.32) | collective-permute-done | bytes 196640 | tf_op jit(solution)/shard_map/cond/branch_1_fun/ppermute | solution.py:461
  66.9 0.1 collective-permute-start.36
  67.1 2.3 %branch_1_fun.12.column_ref = f32[512,512]{1,0:T(8,128)S(1)} custom-call(s32[2]{0:T(128)S(1)} %get-tuple-element.67.where_ref, s32[96]{0:T(128)S(1)} %get-tuple-element.68.fill_ref, f32[512,512]{1,0:T(8,128)S(1)} %get-tuple-element.89.inverse_ref, f32[6,32,256]{2,1,0:T(8,128)S(1)} %get-tuple-element.130.refs_0_, ...), custom_call_target="tpu_custom_call" | custom-call | tf_op jit(solution)/shard_map/cond/branch_1_fun/pallas_call | solution.py:365
  69.4 3.2 %collective-permute-done.29.refs_10_ = f32[10,32,256]{2,1,0:T(8,128)S(1)} collective-permute-done((f32[10,32,256]{2,1,0:T(8,128)S(1)}, f32[10,32,256]{2,1,0:T(8,128)S(1)}, u32[]{:S(2)}, u32[]{:S(2)}) %collective-permute-start.29) | collective-permute-done | bytes 327712 | tf_op jit(solution)/shard_map/cond/branch_1_fun/ppermute | solution.py:461
  72.6 0.0 collective-permute-start.37
  72.6 0.0 collective-permute-done.33.refs_2_
  72.6 0.0 collective-permute-done.34.refs_5_
  72.6 0.0 collective-permute-done.35.refs_8_
  72.6 1.6 %collective-permute-done.37.refs_12_ = f32[10,32,256]{2,1,0:T(8,128)S(1)} collective-permute-done((f32[10,32,256]{2,1,0:T(8,128)S(1)}, f32[10,32,256]{2,1,0:T(8,128)S(1)}, u32[]{:S(2)}, u32[]{:S(2)}) %collective-permute-start.37) | collective-permute-done | bytes 327712 | tf_op jit(solution)/shard_map/cond/branch_1_fun/ppermute | solution.py:461
  74.2 4.6 %branch_1_fun.13 = f32[3072,512]{1,0:T(8,128)} custom-call(s32[2]{0:T(128)S(1)} %get-tuple-element.67.where_ref, s32[48]{0:T(128)S(1)} %get-tuple-element.85.slot_ref, f32[512,512]{1,0:T(8,128)S(1)} %branch_1_fun.12.column_ref, f32[3072,512]{1,0:T(8,128)S(1)} %get-tuple-element.93.window_ref, f32[10,32,256]{2,1,0:T(8,128)S(1)} %branch_1_fun.7.refs_0_, ...), custom_call_target="tpu_custom_call" | custom-call | tf_op jit(solution)/shard_map/cond/branch_1_fun/pallas_call | solution.py:444
  79.1 0.0 copy-start.1
  79.1 0.9 %copy-done.1 = f32[64,512]{1,0:T(8,128)S(1)} copy-done((f32[64,512]{1,0:T(8,128)S(1)}, f32[64,512]{1,0:T(8,128)}, u32[]{:S(2)}) %copy-start.1) | copy-done | bytes 131096
  (20 shorter events, 0.2 us)
Async XLA Ops:
  0.6 1.8 %copy-start = (f32[64,512]{1,0:T(8,128)S(1)}, f32[64,512]{1,0:T(8,128)}, u32[]{:S(2)}) copy-start(f32[64,512]{1,0:T(8,128)} %param.8) | copy-start | bytes 393220
  0.7 13.9 %copy-start.11 = (s32[48,2]{0,1:T(2,128)S(1)}, s32[48,2]{0,1:T(2,128)}, u32[]{:S(2)}) copy-start(s32[48,2]{0,1:T(2,128)} %param.9) | copy-start | bytes 1156
  1.9 17.4 %copy-start.6 = (f32[384,512]{1,0:T(8,128)S(1)}, f32[384,512]{1,0:T(8,128)}, u32[]{:S(2)}) copy-start(f32[384,512]{1,0:T(8,128)} %param.7) | copy-start | bytes 2359300
  1.9 5.1 %collective-permute-start.38 = (f32[3,2,32,512]{3,2,1,0:T(8,128)S(1)}, f32[3,2,32,512]{3,2,1,0:T(8,128)S(1)}, u32[]{:S(2)}, u32[]{:S(2)}) collective-permute-start(f32[3,2,32,512]{3,2,1,0:T(8,128)S(1)} %get-tuple-element.132), channel_id=1, source_target_pairs={{0,1},{1,0},{2,3},{3,2},{4,5},{5,4},{6,7},{7,6},{8,9},{9,8},{10,11... | collective-permute-start | bytes 1179656 | tf_op jit(solution)/shard_map/ppermute | solution.py:461
  2.5 4.5 %collective-permute-start.39 = (f32[1,16,512]{2,1,0:T(8,128)S(1)}, f32[1,16,512]{2,1,0:T(8,128)S(1)}, u32[]{:S(2)}, u32[]{:S(2)}) collective-permute-start(f32[1,16,512]{2,1,0:T(8,128)S(1)} %dynamic-slice_bitcast_fusion.6), channel_id=1, source_target_pairs={{0,4},{4,0},{8,12},{12,8},{16,20},{20,16},{24,28},{28,24},{1,5},{5... | collective-permute-start | bytes 98312 | tf_op jit(solution)/shard_map/ppermute | solution.py:461
  7.0 4.4 %collective-permute-start.41 = (f32[2,16,512]{2,1,0:T(8,128)S(1)}, f32[2,16,512]{2,1,0:T(8,128)S(1)}, u32[]{:S(2)}, u32[]{:S(2)}) collective-permute-start(f32[2,16,512]{2,1,0:T(8,128)S(1)} %maximum_select_fusion.1), channel_id=1, source_target_pairs={{0,8},{4,12},{8,0},{12,4},{16,24},{20,28},{24,16},{28,20},{1,9},{5... | collective-permute-start | bytes 196616 | tf_op jit(solution)/shard_map/ppermute | solution.py:461
  9.2 10.1 %collective-permute-start.40 = (f32[2,3,32,512]{3,2,1,0:T(8,128)S(1)}, f32[2,3,32,512]{3,2,1,0:T(8,128)S(1)}, u32[]{:S(2)}, u32[]{:S(2)}) collective-permute-start(f32[2,3,32,512]{3,2,1,0:T(8,128)S(1)} %fusion.1), channel_id=1, source_target_pairs={{0,4},{4,0},{8,12},{12,8},{16,20},{20,16},{24,28},{28,24},{1,5},{5... | collective-permute-start | bytes 1179656 | tf_op jit(solution)/shard_map/ppermute | solution.py:461
  11.4 7.8 %collective-permute-start.42 = (f32[4,16,512]{2,1,0:T(8,128)S(1)}, f32[4,16,512]{2,1,0:T(8,128)S(1)}, u32[]{:S(2)}, u32[]{:S(2)}) collective-permute-start(f32[4,16,512]{2,1,0:T(8,128)S(1)} %maximum_select_fusion), channel_id=1, source_target_pairs={{0,16},{4,20},{8,24},{12,28},{16,0},{20,4},{24,8},{28,12},{1,17},{... | collective-permute-start | bytes 393224 | tf_op jit(solution)/shard_map/ppermute | solution.py:461
  19.5 2.6 %copy-start.9 = (f32[384,512]{1,0:T(8,128)}, f32[384,512]{1,0:T(8,128)S(1)}, u32[]{:S(2)}) copy-start(f32[384,512]{1,0:T(8,128)S(1)} %get-tuple-element.82.panel_ref) | copy-start | bytes 2359300 | tf_op jit(solution)/shard_map/cond
  19.6 7.6 %collective-permute-start.22 = (f32[8,16,512]{2,1,0:T(8,128)S(1)}, f32[8,16,512]{2,1,0:T(8,128)S(1)}, u32[]{:S(2)}, u32[]{:S(2)}) collective-permute-start(f32[8,16,512]{2,1,0:T(8,128)S(1)} %broadcast_select_fusion.3.refs_0_), channel_id=1, source_target_pairs={{0,2},{1,3},{2,0},{3,1},{4,6},{5,7},{6,4},{7,5},{8,10},{9,11},{10,... | collective-permute-start | bytes 786440 | tf_op jit(solution)/shard_map/cond/branch_1_fun/ppermute | solution.py:461
  22.1 7.1 %collective-permute-start.20 = (f32[10,32,256]{2,1,0:T(8,128)S(1)}, f32[10,32,256]{2,1,0:T(8,128)S(1)}, u32[]{:S(2)}, u32[]{:S(2)}) collective-permute-start(f32[10,32,256]{2,1,0:T(8,128)S(1)} %branch_1_fun.7.refs_0_), channel_id=1, source_target_pairs={{0,4},{4,0},{8,12},{12,8},{16,20},{20,16},{24,28},{28,24},{1,5},{5... | collective-permute-start | bytes 983048 | tf_op jit(solution)/shard_map/cond/branch_1_fun/ppermute | solution.py:461
  23.7 11.0 %collective-permute-start.19 = (f32[10,32,256]{2,1,0:T(8,128)S(1)}, f32[10,32,256]{2,1,0:T(8,128)S(1)}, u32[]{:S(2)}, u32[]{:S(2)}) collective-permute-start(f32[10,32,256]{2,1,0:T(8,128)S(1)} %branch_1_fun.7.refs_0_), channel_id=1, source_target_pairs={{0,24},{4,28},{8,0},{12,4},{16,8},{20,12},{24,16},{28,20},{1,25},{... | collective-permute-start | bytes 983048 | tf_op jit(solution)/shard_map/cond/branch_1_fun/ppermute | solution.py:475
  27.1 1.5 %collective-permute-start.21 = (f32[8,16,512]{2,1,0:T(8,128)S(1)}, f32[8,16,512]{2,1,0:T(8,128)S(1)}, u32[]{:S(2)}, u32[]{:S(2)}) collective-permute-start(f32[8,16,512]{2,1,0:T(8,128)S(1)} %broadcast_select_fusion.3.refs_0_), channel_id=1, source_target_pairs={{0,1},{1,0},{2,3},{3,2},{4,5},{5,4},{6,7},{7,6},{8,9},{9,8},{10,11... | collective-permute-start | bytes 786440 | tf_op jit(solution)/shard_map/cond/branch_1_fun/ppermute | solution.py:461
  27.2 7.5 %collective-permute-start.23 = (f32[8,16,512]{2,1,0:T(8,128)S(1)}, f32[8,16,512]{2,1,0:T(8,128)S(1)}, u32[]{:S(2)}, u32[]{:S(2)}) collective-permute-start(f32[8,16,512]{2,1,0:T(8,128)S(1)} %collective-permute-done.22.refs_2_), channel_id=1, source_target_pairs={{0,1},{1,0},{2,3},{3,2},{4,5},{5,4},{6,7},{7,6},{8,9},{9,8},{10,11... | collective-permute-start | bytes 786440 | tf_op jit(solution)/shard_map/cond/branch_1_fun/ppermute | solution.py:461
  27.7 17.6 %collective-permute-start.25 = (f32[10,32,256]{2,1,0:T(8,128)S(1)}, f32[10,32,256]{2,1,0:T(8,128)S(1)}, u32[]{:S(2)}, u32[]{:S(2)}) collective-permute-start(f32[10,32,256]{2,1,0:T(8,128)S(1)} %branch_1_fun.7.refs_0_), channel_id=1, source_target_pairs={{0,16},{4,20},{8,24},{12,28},{16,0},{20,4},{24,8},{28,12},{1,17},{... | collective-permute-start | bytes 983048 | tf_op jit(solution)/shard_map/cond/branch_1_fun/ppermute | solution.py:475
  34.7 10.6 %collective-permute-start.24 = (f32[10,32,256]{2,1,0:T(8,128)S(1)}, f32[10,32,256]{2,1,0:T(8,128)S(1)}, u32[]{:S(2)}, u32[]{:S(2)}) collective-permute-start(f32[10,32,256]{2,1,0:T(8,128)S(1)} %collective-permute-done.19.refs_1_.refs_3_), channel_id=1, source_target_pairs={{0,4},{4,0},{8,12},{12,8},{16,20},{20,16},{24,28},{28,24},{1,5},{5... | collective-permute-start | bytes 983048 | tf_op jit(solution)/shard_map/cond/branch_1_fun/ppermute | solution.py:461
  46.6 10.5 %collective-permute-start.26 = (f32[2,6,32,256]{3,2,1,0:T(8,128)S(1)}, f32[2,6,32,256]{3,2,1,0:T(8,128)}, u32[]{:S(2)}, u32[]{:S(2)}) collective-permute-start(f32[2,6,32,256]{3,2,1,0:T(8,128)S(1)} %branch_1_fun.10), channel_id=1, source_target_pairs={{0,2},{1,3},{4,6},{5,7},{8,10},{9,11},{12,14},{13,15},{16,18},{17,... | collective-permute-start | bytes 1179656 | tf_op jit(solution)/shard_map/cond/branch_1_fun/ppermute | solution.py:486
  49.7 2.7 %copy-start.10 = (f32[384,512]{1,0:T(8,128)S(1)}, f32[384,512]{1,0:T(8,128)}, u32[]{:S(2)}) copy-start(f32[384,512]{1,0:T(8,128)} %copy-done.9) | copy-start | bytes 2359300 | tf_op jit(solution)/shard_map/cond
  49.7 12.7 %collective-permute-start.28 = (f32[10,32,256]{2,1,0:T(8,128)S(1)}, f32[10,32,256]{2,1,0:T(8,128)S(1)}, u32[]{:S(2)}, u32[]{:S(2)}) collective-permute-start(f32[10,32,256]{2,1,0:T(8,128)S(1)} %collective-permute-done.25.refs_0_.refs_6_), channel_id=1, source_target_pairs={{0,4},{4,0},{8,12},{12,8},{16,20},{20,16},{24,28},{28,24},{1,5},{5... | collective-permute-start | bytes 983048 | tf_op jit(solution)/shard_map/cond/branch_1_fun/ppermute | solution.py:461
  51.0 11.4 %collective-permute-start.27 = (f32[10,32,256]{2,1,0:T(8,128)S(1)}, f32[10,32,256]{2,1,0:T(8,128)S(1)}, u32[]{:S(2)}, u32[]{:S(2)}) collective-permute-start(f32[10,32,256]{2,1,0:T(8,128)S(1)} %branch_1_fun.7.refs_0_), channel_id=1, source_target_pairs={{0,8},{4,12},{8,16},{12,20},{16,24},{20,28},{24,0},{28,4},{1,9},{5... | collective-permute-start | bytes 983048 | tf_op jit(solution)/shard_map/cond/branch_1_fun/ppermute | solution.py:475
  52.3 20.3 %collective-permute-start.33 = (f32[2,10,32,256]{3,2,1,0:T(8,128)S(1)}, f32[2,10,32,256]{3,2,1,0:T(8,128)S(1)}, u32[]{:S(2)}, u32[]{:S(2)}) collective-permute-start(f32[2,10,32,256]{3,2,1,0:T(8,128)S(1)} %pad_maximum_fusion.3), channel_id=1, source_target_pairs={{0,1},{1,0},{2,3},{3,2},{4,5},{5,4},{6,7},{7,6},{8,9},{9,8},{10,11... | collective-permute-start | bytes 1966088 | tf_op jit(solution)/shard_map/cond/branch_1_fun/ppermute | solution.py:461
  57.2 7.4 %collective-permute-start.31 = (f32[6,32,256]{2,1,0:T(8,128)S(1)}, f32[6,32,256]{2,1,0:T(8,128)S(1)}, u32[]{:S(2)}, u32[]{:S(2)}) collective-permute-start(f32[6,32,256]{2,1,0:T(8,128)S(1)} %get-tuple-element.129), channel_id=1, source_target_pairs={{0,4},{4,0},{8,12},{12,8},{16,20},{20,16},{24,28},{28,24},{1,5},{5... | collective-permute-start | bytes 589832 | tf_op jit(solution)/shard_map/cond/branch_1_fun/ppermute | solution.py:461
  58.8 13.8 %collective-permute-start.34 = (f32[2,10,32,256]{3,2,1,0:T(8,128)S(1)}, f32[2,10,32,256]{3,2,1,0:T(8,128)S(1)}, u32[]{:S(2)}, u32[]{:S(2)}) collective-permute-start(f32[2,10,32,256]{3,2,1,0:T(8,128)S(1)} %pad_maximum_fusion.4), channel_id=1, source_target_pairs={{0,1},{1,0},{2,3},{3,2},{4,5},{5,4},{6,7},{7,6},{8,9},{9,8},{10,11... | collective-permute-start | bytes 1966088 | tf_op jit(solution)/shard_map/cond/branch_1_fun/ppermute | solution.py:461
  62.4 2.1 %collective-permute-start.30 = (f32[6,32,256]{2,1,0:T(8,128)S(1)}, f32[6,32,256]{2,1,0:T(8,128)S(1)}, u32[]{:S(2)}, u32[]{:S(2)}) collective-permute-start(f32[6,32,256]{2,1,0:T(8,128)S(1)} %get-tuple-element.130.refs_0_), channel_id=1, source_target_pairs={{0,1},{1,0},{2,3},{3,2},{4,5},{5,4},{6,7},{7,6},{8,9},{9,8},{10,11... | collective-permute-start | bytes 589832 | tf_op jit(solution)/shard_map/cond/branch_1_fun/ppermute | solution.py:461
  62.4 10.1 %collective-permute-start.29 = (f32[10,32,256]{2,1,0:T(8,128)S(1)}, f32[10,32,256]{2,1,0:T(8,128)S(1)}, u32[]{:S(2)}, u32[]{:S(2)}) collective-permute-start(f32[10,32,256]{2,1,0:T(8,128)S(1)} %collective-permute-done.27.refs_9_), channel_id=1, source_target_pairs={{0,4},{4,0},{8,12},{12,8},{16,20},{20,16},{24,28},{28,24},{1,5},{5... | collective-permute-start | bytes 983048 | tf_op jit(solution)/shard_map/cond/branch_1_fun/ppermute | solution.py:461
  64.5 8.1 %collective-permute-start.35 = (f32[2,10,32,256]{3,2,1,0:T(8,128)S(1)}, f32[2,10,32,256]{3,2,1,0:T(8,128)S(1)}, u32[]{:S(2)}, u32[]{:S(2)}) collective-permute-start(f32[2,10,32,256]{3,2,1,0:T(8,128)S(1)} %pad_maximum_fusion.5), channel_id=1, source_target_pairs={{0,1},{1,0},{2,3},{3,2},{4,5},{5,4},{6,7},{7,6},{8,9},{9,8},{10,11... | collective-permute-start | bytes 1966088 | tf_op jit(solution)/shard_map/cond/branch_1_fun/ppermute | solution.py:461
  64.5 2.4 %collective-permute-start.32 = (f32[6,32,256]{2,1,0:T(8,128)S(1)}, f32[6,32,256]{2,1,0:T(8,128)S(1)}, u32[]{:S(2)}, u32[]{:S(2)}) collective-permute-start(f32[6,32,256]{2,1,0:T(8,128)S(1)} %collective-permute-done.31.refs_2_), channel_id=1, source_target_pairs={{0,1},{1,0},{2,3},{3,2},{4,5},{5,4},{6,7},{7,6},{8,9},{9,8},{10,11... | collective-permute-start | bytes 589832 | tf_op jit(solution)/shard_map/cond/branch_1_fun/ppermute | solution.py:461
  66.9 5.7 %collective-permute-start.36 = (f32[10,32,256]{2,1,0:T(8,128)S(1)}, f32[10,32,256]{2,1,0:T(8,128)S(1)}, u32[]{:S(2)}, u32[]{:S(2)}) collective-permute-start(f32[10,32,256]{2,1,0:T(8,128)S(1)} %collective-permute-done.27.refs_9_), channel_id=1, source_target_pairs={{0,1},{1,0},{2,3},{3,2},{4,5},{5,4},{6,7},{7,6},{8,9},{9,8},{10,11... | collective-permute-start | bytes 983048 | tf_op jit(solution)/shard_map/cond/branch_1_fun/ppermute | solution.py:461
  72.6 1.6 %collective-permute-start.37 = (f32[10,32,256]{2,1,0:T(8,128)S(1)}, f32[10,32,256]{2,1,0:T(8,128)S(1)}, u32[]{:S(2)}, u32[]{:S(2)}) collective-permute-start(f32[10,32,256]{2,1,0:T(8,128)S(1)} %collective-permute-done.29.refs_10_), channel_id=1, source_target_pairs={{0,1},{1,0},{2,3},{3,2},{4,5},{5,4},{6,7},{7,6},{8,9},{9,8},{10,11... | collective-permute-start | bytes 983048 | tf_op jit(solution)/shard_map/cond/branch_1_fun/ppermute | solution.py:461
  79.1 0.9 %copy-start.1 = (f32[64,512]{1,0:T(8,128)S(1)}, f32[64,512]{1,0:T(8,128)}, u32[]{:S(2)}) copy-start(f32[64,512]{1,0:T(8,128)} %param.8) | copy-start | bytes 393220

commit v2 on v0

--- a/solution.py
+++ b/solution.py
@@ -523,6 +523,7 @@
         later = [s for s in range(1, sizes.groups) if s not in sizes.needed]
         lists |= {s: bring(sizes, own, s) for s in first}
         sides = {0: swap(own, "col", 1)}
+        pivot, own = lax.optimization_barrier((pivot, own))
         parts = [pivot] + ([swap(pivot, "row", 2)] if split == 4 else [])
         parts = [part for value in parts for part in (value, swap(value, "row", 1))]
         near = first[0]

time: 79.8 us -> 80.5 us (level)
  waiting for transfers between devices: 22.3 us -> 23.5 us
    ppermute x20, waiting for transfers between devices: 15.4 us -> 16.4 us  [swap(): return lax.ppermute(value, axis, [(i, i ^ step) for i in range(size)])]
  transfers between devices with their start and end apart: 24 -> 24, of which waited for: 12 -> 11; matrix products, arithmetic and copies ran while one was open for 1% -> 1% of each run, Pallas kernels for 22% -> 21%
where the time goes in v2:
time: 80.5 us; the launch traced here: 80.3 us
  starting transfers between devices  29.6 us (37%)
  waiting for transfers between devices  23.5 us (29%)
  Pallas kernels  22.2 us (28%)
  local copies, waits for them, and re-layouts  2.41 us (3%)
  between operations  1.41 us (2%)
    ppermute x20, starting transfers between devices, swap(): return lax.ppermute(value, axis, [(i, i ^ step) for i in range(size)])  17.9 us
    ppermute x20, waiting for transfers between devices, swap(): return lax.ppermute(value, axis, [(i, i ^ step) for i in range(size)])  16.4 us
    ppermute x3, starting transfers between devices, bring(): return lax.ppermute(value, 'col', pairs)  7.54 us
    ppermute x3, waiting for transfers between devices, bring(): return lax.ppermute(value, 'col', pairs)  7.12 us
    pallas_call x1, Pallas kernels, inverse_factor(): pl.pallas_call(inverse_factor_kernel, out_shape=jax.ShapeDtypeStruct((n,...  6.9 us
    pallas_call x1, Pallas kernels, own_factor(): pl.pallas_call(functools.partial(own_factor_kernel, sizes), out_shape=(pl...  4.63 us
    ppermute x1, starting transfers between devices, spread_column(): other = lax.ppermute(value, ('col', 'row'), pairs)  4.18 us
    pallas_call x1, Pallas kernels, update(): pl.pallas_call(functools.partial(update_kernel, sizes, [len(group) for gr...  3.34 us
  transfers between devices with their start and end apart: 24, of which 11 were waited for; matrix products, arithmetic and copies ran while one was open for 1% of the time, Pallas kernels for 21%

profile of v2, /device:TPU:0, one launch (start us, length us, event | category | flops | bytes accessed | tf_op | source)
XLA Modules:
  0.0 80.3 jit_solution(11726633377590793562)
XLA Ops:
  0.6 0.0 copy-start
  0.7 1.2 %dynamic-slice_bitcast_fusion.4 = (f32[1,3,2,32,512]{4,3,2,1,0:T(8,128)S(1)}, f32[3,2,32,512]{3,2,1,0:T(8,128)S(1)}) fusion(f32[3,2,2,32,512]{4,3,2,1,0:T(8,128)} %bitcast.50, s32[]{:T(128)S(6)} %select_n.102, s32[]{:T(128)S(6)} %select_n.97), kind=kLoop, calls=%fused_computation.18 | loop fusion | bytes 1572872 | tf_op jit(solution)/shard_map/stack | solution.py:512
  1.9 0.0 copy-start.6
  1.9 0.5 collective-permute-start.38
  2.5 2.6 %collective-permute-start.39 = (f32[1,16,512]{2,1,0:T(8,128)S(1)}, f32[1,16,512]{2,1,0:T(8,128)S(1)}, u32[]{:S(2)}, u32[]{:S(2)}) collective-permute-start(f32[1,16,512]{2,1,0:T(8,128)S(1)} %dynamic-slice_bitcast_fusion.6), channel_id=1, source_target_pairs={{0,4},{4,0},{8,12},{12,8},{16,20},{20,16},{24,28},{28,24},{1,5},{5... | collective-permute-start | bytes 98312 | tf_op jit(solution)/shard_map/ppermute | solution.py:461
  5.1 1.9 %collective-permute-done.39 = f32[1,16,512]{2,1,0:T(8,128)S(1)} collective-permute-done((f32[1,16,512]{2,1,0:T(8,128)S(1)}, f32[1,16,512]{2,1,0:T(8,128)S(1)}, u32[]{:S(2)}, u32[]{:S(2)}) %collective-permute-start.39) | collective-permute-done | bytes 32800 | tf_op jit(solution)/shard_map/ppermute | solution.py:461
  7.0 0.0 collective-permute-done.38
  7.0 2.2 %collective-permute-start.41 = (f32[2,16,512]{2,1,0:T(8,128)S(1)}, f32[2,16,512]{2,1,0:T(8,128)S(1)}, u32[]{:S(2)}, u32[]{:S(2)}) collective-permute-start(f32[2,16,512]{2,1,0:T(8,128)S(1)} %maximum_select_fusion.1), channel_id=1, source_target_pairs={{0,8},{4,12},{8,0},{12,4},{16,24},{20,28},{24,16},{28,20},{1,9},{5... | collective-permute-start | bytes 196616 | tf_op jit(solution)/shard_map/ppermute | solution.py:461
  9.2 1.6 %collective-permute-start.40 = (f32[2,3,32,512]{3,2,1,0:T(8,128)S(1)}, f32[2,3,32,512]{3,2,1,0:T(8,128)S(1)}, u32[]{:S(2)}, u32[]{:S(2)}) collective-permute-start(f32[2,3,32,512]{3,2,1,0:T(8,128)S(1)} %fusion.1), channel_id=1, source_target_pairs={{0,4},{4,0},{8,12},{12,8},{16,20},{20,16},{24,28},{28,24},{1,5},{5... | collective-permute-start | bytes 1179656 | tf_op jit(solution)/shard_map/ppermute | solution.py:461
  10.8 0.7 collective-permute-done.41
  11.4 3.1 %collective-permute-start.42 = (f32[4,16,512]{2,1,0:T(8,128)S(1)}, f32[4,16,512]{2,1,0:T(8,128)S(1)}, u32[]{:S(2)}, u32[]{:S(2)}) collective-permute-start(f32[4,16,512]{2,1,0:T(8,128)S(1)} %maximum_select_fusion), channel_id=1, source_target_pairs={{0,16},{4,20},{8,24},{12,28},{16,0},{20,4},{24,8},{28,12},{1,17},{... | collective-permute-start | bytes 393224 | tf_op jit(solution)/shard_map/ppermute | solution.py:461
  14.5 0.1 copy.13
  14.6 0.1 reshape.18.fill_ref
  14.7 1.2 %shard_map.63 = s32[1]{0:T(128)} custom-call(s32[96]{0:T(128)S(1)} %reshape.18.fill_ref), custom_call_target="tpu_custom_call" | custom-call | tf_op jit(solution)/shard_map/pallas_call | solution.py:186
  16.6 0.1 pad_add_fusion
  16.7 2.5 %collective-permute-done.42 = f32[4,16,512]{2,1,0:T(8,128)S(1)} collective-permute-done((f32[4,16,512]{2,1,0:T(8,128)S(1)}, f32[4,16,512]{2,1,0:T(8,128)S(1)}, u32[]{:S(2)}, u32[]{:S(2)}) %collective-permute-start.42) | collective-permute-done | bytes 131104 | tf_op jit(solution)/shard_map/ppermute | solution.py:461
  19.2 0.1 pad_maximum_fusion.7
  19.3 0.0 collective-permute-done.40
  19.3 60.1 %conditional.1 = (f32[384,512]{1,0:T(8,128)}, f32[3072,512]{1,0:T(8,128)}) conditional(s32[]{:T(128)} %bitcast.18, (s32[2]{0:T(128)S(1)}, s32[96]{0:T(128)S(1)}, f32[384,512]{1,0:T(8,128)S(1)}, f32[3,2,32,512]{3,2,1,0:T(8,128)S(1)}, f32[2,3,32,512]{3,2,1,0:T(8,128)S(1)}, /*index=5*/s32[]{:T(128)}, f32[384,512]{1,0:T(8,128)S(1)}, ...), branch_computations={%region_0.1_spmd, %region_1.2_spmd} | conditional | flops 1376297 | bytes 87295320 | solution.py:568
  19.5 0.0 copy-start.9
  19.6 0.9 %branch_1_fun.7.refs_0_ = f32[10,32,256]{2,1,0:T(8,128)S(1)} custom-call(s32[2]{0:T(128)S(1)} %get-tuple-element.67.where_ref, s32[96]{0:T(128)S(1)} %get-tuple-element.68.fill_ref, f32[3,128,512]{2,1,0:T(8,128)S(1)} %bitcast.52, f32[3,2,32,512]{3,2,1,0:T(8,128)S(1)} %get-tuple-element.70.core_ref, f32[2,3,32,512]{3,2,1,0:T(8,128)S(1)} %get-tuple-element.71.side_ref), custom_call_target="tpu_custom_call" | custom-call | tf_op jit(solution)/shard_map/cond/branch_1_fun/pallas_call | solution.py:221
  20.5 1.6 %collective-permute-start.21 = (f32[8,16,512]{2,1,0:T(8,128)S(1)}, f32[8,16,512]{2,1,0:T(8,128)S(1)}, u32[]{:S(2)}, u32[]{:S(2)}) collective-permute-start(f32[8,16,512]{2,1,0:T(8,128)S(1)} %broadcast_select_fusion.3.refs_0_), channel_id=1, source_target_pairs={{0,2},{1,3},{2,0},{3,1},{4,6},{5,7},{6,4},{7,5},{8,10},{9,11},{10,... | collective-permute-start | bytes 786440 | tf_op jit(solution)/shard_map/cond/branch_1_fun/ppermute | solution.py:461
  22.1 3.5 %collective-permute-start.19 = (f32[10,32,256]{2,1,0:T(8,128)S(1)}, f32[10,32,256]{2,1,0:T(8,128)S(1)}, u32[]{:S(2)}, u32[]{:S(2)}) collective-permute-start(f32[10,32,256]{2,1,0:T(8,128)S(1)} %branch_1_fun.7.refs_0_), channel_id=1, source_target_pairs={{0,24},{4,28},{8,0},{12,4},{16,8},{20,12},{24,16},{28,20},{1,25},{... | collective-permute-start | bytes 983048 | tf_op jit(solution)/shard_map/cond/branch_1_fun/ppermute | solution.py:475
  25.6 0.0 collective-permute-start.20
  25.6 1.4 %collective-permute-done.21.refs_2_ = f32[8,16,512]{2,1,0:T(8,128)S(1)} collective-permute-done((f32[8,16,512]{2,1,0:T(8,128)S(1)}, f32[8,16,512]{2,1,0:T(8,128)S(1)}, u32[]{:S(2)}, u32[]{:S(2)}) %collective-permute-start.21) | collective-permute-done | bytes 262176 | tf_op jit(solution)/shard_map/cond/branch_1_fun/ppermute | solution.py:461
  26.9 0.0 collective-permute-start.22
  27.0 2.3 %collective-permute-start.25 = (f32[10,32,256]{2,1,0:T(8,128)S(1)}, f32[10,32,256]{2,1,0:T(8,128)S(1)}, u32[]{:S(2)}, u32[]{:S(2)}) collective-permute-start(f32[10,32,256]{2,1,0:T(8,128)S(1)} %branch_1_fun.7.refs_0_), channel_id=1, source_target_pairs={{0,16},{4,20},{8,24},{12,28},{16,0},{20,4},{24,8},{28,12},{1,17},{... | collective-permute-start | bytes 983048 | tf_op jit(solution)/shard_map/cond/branch_1_fun/ppermute | solution.py:475
  29.2 1.5 %collective-permute-start.23 = (f32[10,32,256]{2,1,0:T(8,128)S(1)}, f32[10,32,256]{2,1,0:T(8,128)S(1)}, u32[]{:S(2)}, u32[]{:S(2)}) collective-permute-start(f32[10,32,256]{2,1,0:T(8,128)S(1)} %branch_1_fun.7.refs_0_), channel_id=1, source_target_pairs={{0,4},{4,0},{8,12},{12,8},{16,20},{20,16},{24,28},{28,24},{1,5},{5... | collective-permute-start | bytes 983048 | tf_op jit(solution)/shard_map/cond/branch_1_fun/ppermute | solution.py:461
  30.7 0.0 collective-permute-done.20.refs_1_
  30.7 0.0 collective-permute-done.19.refs_1_.refs_3_
  30.7 0.0 collective-permute-done.22.refs_3_
  30.7 1.2 %collective-permute-start.24 = (f32[10,32,256]{2,1,0:T(8,128)S(1)}, f32[10,32,256]{2,1,0:T(8,128)S(1)}, u32[]{:S(2)}, u32[]{:S(2)}) collective-permute-start(f32[10,32,256]{2,1,0:T(8,128)S(1)} %collective-permute-done.19.refs_1_.refs_3_), channel_id=1, source_target_pairs={{0,4},{4,0},{8,12},{12,8},{16,20},{20,16},{24,28},{28,24},{1,5},{5... | collective-permute-start | bytes 983048 | tf_op jit(solution)/shard_map/cond/branch_1_fun/ppermute | solution.py:461
  32.0 1.6 %branch_1_fun.9.refs_1_ = f32[2,6,32,256]{3,2,1,0:T(8,128)S(1)} custom-call(s32[2]{0:T(128)S(1)} %get-tuple-element.67.where_ref, s32[96]{0:T(128)S(1)} %get-tuple-element.68.fill_ref, f32[10,32,256]{2,1,0:T(8,128)S(1)} %branch_1_fun.7.refs_0_, f32[10,32,256]{2,1,0:T(8,128)S(1)} %collective-permute-done.19.refs_1_.refs_3_), custom_call_target="tpu_custom_call" | custom-call | tf_op jit(solution)/shard_map/cond/branch_1_fun/pallas_call | solution.py:269
  33.6 6.9 %branch_1_fun.8.w_ref = f32[512,512]{1,0:T(8,128)S(1)} custom-call(s32[2]{0:T(128)S(1)} %get-tuple-element.67.where_ref, f32[8,16,512]{2,1,0:T(8,128)S(1)} %broadcast_select_fusion.3.refs_0_, f32[8,16,512]{2,1,0:T(8,128)S(1)} %collective-permute-done.20.refs_1_, f32[8,16,512]{2,1,0:T(8,128)S(1)} %collective-permute-done.21.refs_2_, ...), custom_call_target="tpu_custom_call" | custom-call | tf_op jit(solution)/shard_map/cond/branch_1_fun/pallas_call | solution.py:106
  40.5 4.5 %collective-permute-done.25.refs_0_.refs_6_ = f32[10,32,256]{2,1,0:T(8,128)S(1)} collective-permute-done((f32[10,32,256]{2,1,0:T(8,128)S(1)}, f32[10,32,256]{2,1,0:T(8,128)S(1)}, u32[]{:S(2)}, u32[]{:S(2)}) %collective-permute-start.25) | collective-permute-done | bytes 327712 | tf_op jit(solution)/shard_map/cond/branch_1_fun/ppermute | solution.py:475
  45.0 0.0 collective-permute-done.23.refs_1_
  45.0 1.1 %collective-permute-done.24.refs_4_ = f32[10,32,256]{2,1,0:T(8,128)S(1)} collective-permute-done((f32[10,32,256]{2,1,0:T(8,128)S(1)}, f32[10,32,256]{2,1,0:T(8,128)S(1)}, u32[]{:S(2)}, u32[]{:S(2)}) %collective-permute-start.24) | collective-permute-done | bytes 327712 | tf_op jit(solution)/shard_map/cond/branch_1_fun/ppermute | solution.py:461
  46.1 1.3 %branch_1_fun.10 = f32[2,6,32,256]{3,2,1,0:T(8,128)S(1)} custom-call(s32[2]{0:T(128)S(1)} %get-tuple-element.67.where_ref, s32[96]{0:T(128)S(1)} %get-tuple-element.68.fill_ref, f32[10,32,256]{2,1,0:T(8,128)S(1)} %collective-permute-done.25.refs_0_.refs_6_, f32[2,6,32,256]{3,2,1,0:T(8,128)S(1)} %branch_1_fun.9.refs_1_), custom_call_target="tpu_custom_call" | custom-call | tf_op jit(solution)/shard_map/cond/branch_1_fun/pallas_call | solution.py:269
  47.4 4.2 %collective-permute-start.26 = (f32[2,6,32,256]{3,2,1,0:T(8,128)S(1)}, f32[2,6,32,256]{3,2,1,0:T(8,128)}, u32[]{:S(2)}, u32[]{:S(2)}) collective-permute-start(f32[2,6,32,256]{3,2,1,0:T(8,128)S(1)} %branch_1_fun.10), channel_id=1, source_target_pairs={{0,2},{1,3},{4,6},{5,7},{8,10},{9,11},{12,14},{13,15},{16,18},{17,... | collective-permute-start | bytes 1179656 | tf_op jit(solution)/shard_map/cond/branch_1_fun/ppermute | solution.py:486
  51.5 1.5 %collective-permute-start.28 = (f32[10,32,256]{2,1,0:T(8,128)S(1)}, f32[10,32,256]{2,1,0:T(8,128)S(1)}, u32[]{:S(2)}, u32[]{:S(2)}) collective-permute-start(f32[10,32,256]{2,1,0:T(8,128)S(1)} %collective-permute-done.25.refs_0_.refs_6_), channel_id=1, source_target_pairs={{0,4},{4,0},{8,12},{12,8},{16,20},{20,16},{24,28},{28,24},{1,5},{5... | collective-permute-start | bytes 983048 | tf_op jit(solution)/shard_map/cond/branch_1_fun/ppermute | solution.py:461
  53.0 1.8 %collective-permute-start.27 = (f32[10,32,256]{2,1,0:T(8,128)S(1)}, f32[10,32,256]{2,1,0:T(8,128)S(1)}, u32[]{:S(2)}, u32[]{:S(2)}) collective-permute-start(f32[10,32,256]{2,1,0:T(8,128)S(1)} %branch_1_fun.7.refs_0_), channel_id=1, source_target_pairs={{0,8},{4,12},{8,16},{12,20},{16,24},{20,28},{24,0},{28,4},{1,9},{5... | collective-permute-start | bytes 983048 | tf_op jit(solution)/shard_map/cond/branch_1_fun/ppermute | solution.py:475
  54.9 0.1 collective-permute-start.33
  55.0 4.6 %branch_1_fun.11 = (f32[384,512]{1,0:T(8,128)}, s32[48]{0:T(128)S(1)}, f32[3072,512]{1,0:T(8,128)S(1)}, f32[512,512]{1,0:T(8,128)S(1)}) custom-call(s32[2]{0:T(128)S(1)} %get-tuple-element.67.where_ref, s32[96]{0:T(128)S(1)} %get-tuple-element.68.fill_ref, f32[512,512]{1,0:T(8,128)S(1)} %branch_1_fun.8.w_ref, f32[384,512]{1,0:T(8,128)S(1)} %copy-done.10, ...), custom_call_target="tpu_custom_call" | custom-call | tf_op jit(solution)/shard_map/cond/branch_1_fun/pallas_call | solution.py:320
  59.6 0.0 collective-permute-done.26
  59.6 0.1 broadcast_select_fusion.2
  59.7 0.7 collective-permute-start.31
  60.4 0.2 collective-permute-start.34
  60.7 2.6 %collective-permute-done.27.refs_9_ = f32[10,32,256]{2,1,0:T(8,128)S(1)} collective-permute-done((f32[10,32,256]{2,1,0:T(8,128)S(1)}, f32[10,32,256]{2,1,0:T(8,128)S(1)}, u32[]{:S(2)}, u32[]{:S(2)}) %collective-permute-start.27) | collective-permute-done | bytes 327712 | tf_op jit(solution)/shard_map/cond/branch_1_fun/ppermute | solution.py:475
  63.3 0.5 collective-permute-start.29
  63.8 0.1 pad_maximum_fusion.5
  63.9 3.6 %collective-permute-done.31.refs_2_ = f32[6,32,256]{2,1,0:T(8,128)S(1)} collective-permute-done((f32[6,32,256]{2,1,0:T(8,128)S(1)}, f32[6,32,256]{2,1,0:T(8,128)S(1)}, u32[]{:S(2)}, u32[]{:S(2)}) %collective-permute-start.31) | collective-permute-done | bytes 196640 | tf_op jit(solution)/shard_map/cond/branch_1_fun/ppermute | solution.py:461
  67.5 0.5 collective-permute-start.32
  68.0 1.9 %collective-permute-done.32.refs_3_ = f32[6,32,256]{2,1,0:T(8,128)S(1)} collective-permute-done((f32[6,32,256]{2,1,0:T(8,128)S(1)}, f32[6,32,256]{2,1,0:T(8,128)S(1)}, u32[]{:S(2)}, u32[]{:S(2)}) %collective-permute-start.32) | collective-permute-done | bytes 196640 | tf_op jit(solution)/shard_map/cond/branch_1_fun/ppermute | solution.py:461
  69.9 0.1 collective-permute-start.36
  70.0 2.3 %branch_1_fun.12.column_ref = f32[512,512]{1,0:T(8,128)S(1)} custom-call(s32[2]{0:T(128)S(1)} %get-tuple-element.67.where_ref, s32[96]{0:T(128)S(1)} %get-tuple-element.68.fill_ref, f32[512,512]{1,0:T(8,128)S(1)} %get-tuple-element.89.inverse_ref, f32[6,32,256]{2,1,0:T(8,128)S(1)} %get-tuple-element.130.refs_0_, ...), custom_call_target="tpu_custom_call" | custom-call | tf_op jit(solution)/shard_map/cond/branch_1_fun/pallas_call | solution.py:365
  72.3 1.8 %collective-permute-done.29.refs_10_ = f32[10,32,256]{2,1,0:T(8,128)S(1)} collective-permute-done((f32[10,32,256]{2,1,0:T(8,128)S(1)}, f32[10,32,256]{2,1,0:T(8,128)S(1)}, u32[]{:S(2)}, u32[]{:S(2)}) %collective-permute-start.29) | collective-permute-done | bytes 327712 | tf_op jit(solution)/shard_map/cond/branch_1_fun/ppermute | solution.py:461
  74.1 0.0 collective-permute-start.37
  74.1 0.0 collective-permute-done.33.refs_2_
  74.1 0.0 collective-permute-done.34.refs_5_
  74.2 0.0 collective-permute-done.35.refs_8_
  74.2 1.6 %collective-permute-done.37.refs_12_ = f32[10,32,256]{2,1,0:T(8,128)S(1)} collective-permute-done((f32[10,32,256]{2,1,0:T(8,128)S(1)}, f32[10,32,256]{2,1,0:T(8,128)S(1)}, u32[]{:S(2)}, u32[]{:S(2)}) %collective-permute-start.37) | collective-permute-done | bytes 327712 | tf_op jit(solution)/shard_map/cond/branch_1_fun/ppermute | solution.py:461
  75.8 3.3 %branch_1_fun.13 = f32[3072,512]{1,0:T(8,128)} custom-call(s32[2]{0:T(128)S(1)} %get-tuple-element.67.where_ref, s32[48]{0:T(128)S(1)} %get-tuple-element.85.slot_ref, f32[512,512]{1,0:T(8,128)S(1)} %branch_1_fun.12.column_ref, f32[3072,512]{1,0:T(8,128)S(1)} %get-tuple-element.93.window_ref, f32[10,32,256]{2,1,0:T(8,128)S(1)} %branch_1_fun.7.refs_0_, ...), custom_call_target="tpu_custom_call" | custom-call | tf_op jit(solution)/shard_map/cond/branch_1_fun/pallas_call | solution.py:444
  79.4 0.0 copy-start.1
  79.4 0.9 %copy-done.1 = f32[64,512]{1,0:T(8,128)S(1)} copy-done((f32[64,512]{1,0:T(8,128)S(1)}, f32[64,512]{1,0:T(8,128)}, u32[]{:S(2)}) %copy-start.1) | copy-done | bytes 131096
  (20 shorter events, 0.2 us)
Async XLA Ops:
  0.6 1.8 %copy-start = (f32[64,512]{1,0:T(8,128)S(1)}, f32[64,512]{1,0:T(8,128)}, u32[]{:S(2)}) copy-start(f32[64,512]{1,0:T(8,128)} %param.8) | copy-start | bytes 393220
  0.7 13.9 %copy-start.11 = (s32[48,2]{0,1:T(2,128)S(1)}, s32[48,2]{0,1:T(2,128)}, u32[]{:S(2)}) copy-start(s32[48,2]{0,1:T(2,128)} %param.9) | copy-start | bytes 1156
  1.9 17.4 %copy-start.6 = (f32[384,512]{1,0:T(8,128)S(1)}, f32[384,512]{1,0:T(8,128)}, u32[]{:S(2)}) copy-start(f32[384,512]{1,0:T(8,128)} %param.7) | copy-start | bytes 2359300
  1.9 5.1 %collective-permute-start.38 = (f32[3,2,32,512]{3,2,1,0:T(8,128)S(1)}, f32[3,2,32,512]{3,2,1,0:T(8,128)S(1)}, u32[]{:S(2)}, u32[]{:S(2)}) collective-permute-start(f32[3,2,32,512]{3,2,1,0:T(8,128)S(1)} %get-tuple-element.132), channel_id=1, source_target_pairs={{0,1},{1,0},{2,3},{3,2},{4,5},{5,4},{6,7},{7,6},{8,9},{9,8},{10,11... | collective-permute-start | bytes 1179656 | tf_op jit(solution)/shard_map/ppermute | solution.py:461
  2.5 4.5 %collective-permute-start.39 = (f32[1,16,512]{2,1,0:T(8,128)S(1)}, f32[1,16,512]{2,1,0:T(8,128)S(1)}, u32[]{:S(2)}, u32[]{:S(2)}) collective-permute-start(f32[1,16,512]{2,1,0:T(8,128)S(1)} %dynamic-slice_bitcast_fusion.6), channel_id=1, source_target_pairs={{0,4},{4,0},{8,12},{12,8},{16,20},{20,16},{24,28},{28,24},{1,5},{5... | collective-permute-start | bytes 98312 | tf_op jit(solution)/shard_map/ppermute | solution.py:461
  7.0 4.4 %collective-permute-start.41 = (f32[2,16,512]{2,1,0:T(8,128)S(1)}, f32[2,16,512]{2,1,0:T(8,128)S(1)}, u32[]{:S(2)}, u32[]{:S(2)}) collective-permute-start(f32[2,16,512]{2,1,0:T(8,128)S(1)} %maximum_select_fusion.1), channel_id=1, source_target_pairs={{0,8},{4,12},{8,0},{12,4},{16,24},{20,28},{24,16},{28,20},{1,9},{5... | collective-permute-start | bytes 196616 | tf_op jit(solution)/shard_map/ppermute | solution.py:461
  9.2 10.1 %collective-permute-start.40 = (f32[2,3,32,512]{3,2,1,0:T(8,128)S(1)}, f32[2,3,32,512]{3,2,1,0:T(8,128)S(1)}, u32[]{:S(2)}, u32[]{:S(2)}) collective-permute-start(f32[2,3,32,512]{3,2,1,0:T(8,128)S(1)} %fusion.1), channel_id=1, source_target_pairs={{0,4},{4,0},{8,12},{12,8},{16,20},{20,16},{24,28},{28,24},{1,5},{5... | collective-permute-start | bytes 1179656 | tf_op jit(solution)/shard_map/ppermute | solution.py:461
  11.4 7.8 %collective-permute-start.42 = (f32[4,16,512]{2,1,0:T(8,128)S(1)}, f32[4,16,512]{2,1,0:T(8,128)S(1)}, u32[]{:S(2)}, u32[]{:S(2)}) collective-permute-start(f32[4,16,512]{2,1,0:T(8,128)S(1)} %maximum_select_fusion), channel_id=1, source_target_pairs={{0,16},{4,20},{8,24},{12,28},{16,0},{20,4},{24,8},{28,12},{1,17},{... | collective-permute-start | bytes 393224 | tf_op jit(solution)/shard_map/ppermute | solution.py:461
  19.5 7.4 %copy-start.9 = (f32[384,512]{1,0:T(8,128)}, f32[384,512]{1,0:T(8,128)S(1)}, u32[]{:S(2)}) copy-start(f32[384,512]{1,0:T(8,128)S(1)} %get-tuple-element.82.panel_ref) | copy-start | bytes 2359300 | tf_op jit(solution)/shard_map/cond
  20.5 6.4 %collective-permute-start.21 = (f32[8,16,512]{2,1,0:T(8,128)S(1)}, f32[8,16,512]{2,1,0:T(8,128)S(1)}, u32[]{:S(2)}, u32[]{:S(2)}) collective-permute-start(f32[8,16,512]{2,1,0:T(8,128)S(1)} %broadcast_select_fusion.3.refs_0_), channel_id=1, source_target_pairs={{0,2},{1,3},{2,0},{3,1},{4,6},{5,7},{6,4},{7,5},{8,10},{9,11},{10,... | collective-permute-start | bytes 786440 | tf_op jit(solution)/shard_map/cond/branch_1_fun/ppermute | solution.py:461
  22.1 8.6 %collective-permute-start.19 = (f32[10,32,256]{2,1,0:T(8,128)S(1)}, f32[10,32,256]{2,1,0:T(8,128)S(1)}, u32[]{:S(2)}, u32[]{:S(2)}) collective-permute-start(f32[10,32,256]{2,1,0:T(8,128)S(1)} %branch_1_fun.7.refs_0_), channel_id=1, source_target_pairs={{0,24},{4,28},{8,0},{12,4},{16,8},{20,12},{24,16},{28,20},{1,25},{... | collective-permute-start | bytes 983048 | tf_op jit(solution)/shard_map/cond/branch_1_fun/ppermute | solution.py:475
  25.6 5.1 %collective-permute-start.20 = (f32[8,16,512]{2,1,0:T(8,128)S(1)}, f32[8,16,512]{2,1,0:T(8,128)S(1)}, u32[]{:S(2)}, u32[]{:S(2)}) collective-permute-start(f32[8,16,512]{2,1,0:T(8,128)S(1)} %broadcast_select_fusion.3.refs_0_), channel_id=1, source_target_pairs={{0,1},{1,0},{2,3},{3,2},{4,5},{5,4},{6,7},{7,6},{8,9},{9,8},{10,11... | collective-permute-start | bytes 786440 | tf_op jit(solution)/shard_map/cond/branch_1_fun/ppermute | solution.py:461
  26.9 3.8 %collective-permute-start.22 = (f32[8,16,512]{2,1,0:T(8,128)S(1)}, f32[8,16,512]{2,1,0:T(8,128)S(1)}, u32[]{:S(2)}, u32[]{:S(2)}) collective-permute-start(f32[8,16,512]{2,1,0:T(8,128)S(1)} %collective-permute-done.21.refs_2_), channel_id=1, source_target_pairs={{0,1},{1,0},{2,3},{3,2},{4,5},{5,4},{6,7},{7,6},{8,9},{9,8},{10,11... | collective-permute-start | bytes 786440 | tf_op jit(solution)/shard_map/cond/branch_1_fun/ppermute | solution.py:461
  27.0 18.0 %collective-permute-start.25 = (f32[10,32,256]{2,1,0:T(8,128)S(1)}, f32[10,32,256]{2,1,0:T(8,128)S(1)}, u32[]{:S(2)}, u32[]{:S(2)}) collective-permute-start(f32[10,32,256]{2,1,0:T(8,128)S(1)} %branch_1_fun.7.refs_0_), channel_id=1, source_target_pairs={{0,16},{4,20},{8,24},{12,28},{16,0},{20,4},{24,8},{28,12},{1,17},{... | collective-permute-start | bytes 983048 | tf_op jit(solution)/shard_map/cond/branch_1_fun/ppermute | solution.py:475
  29.2 15.8 %collective-permute-start.23 = (f32[10,32,256]{2,1,0:T(8,128)S(1)}, f32[10,32,256]{2,1,0:T(8,128)S(1)}, u32[]{:S(2)}, u32[]{:S(2)}) collective-permute-start(f32[10,32,256]{2,1,0:T(8,128)S(1)} %branch_1_fun.7.refs_0_), channel_id=1, source_target_pairs={{0,4},{4,0},{8,12},{12,8},{16,20},{20,16},{24,28},{28,24},{1,5},{5... | collective-permute-start | bytes 983048 | tf_op jit(solution)/shard_map/cond/branch_1_fun/ppermute | solution.py:461
  30.7 15.4 %collective-permute-start.24 = (f32[10,32,256]{2,1,0:T(8,128)S(1)}, f32[10,32,256]{2,1,0:T(8,128)S(1)}, u32[]{:S(2)}, u32[]{:S(2)}) collective-permute-start(f32[10,32,256]{2,1,0:T(8,128)S(1)} %collective-permute-done.19.refs_1_.refs_3_), channel_id=1, source_target_pairs={{0,4},{4,0},{8,12},{12,8},{16,20},{20,16},{24,28},{28,24},{1,5},{5... | collective-permute-start | bytes 983048 | tf_op jit(solution)/shard_map/cond/branch_1_fun/ppermute | solution.py:461
  47.4 12.2 %collective-permute-start.26 = (f32[2,6,32,256]{3,2,1,0:T(8,128)S(1)}, f32[2,6,32,256]{3,2,1,0:T(8,128)}, u32[]{:S(2)}, u32[]{:S(2)}) collective-permute-start(f32[2,6,32,256]{3,2,1,0:T(8,128)S(1)} %branch_1_fun.10), channel_id=1, source_target_pairs={{0,2},{1,3},{4,6},{5,7},{8,10},{9,11},{12,14},{13,15},{16,18},{17,... | collective-permute-start | bytes 1179656 | tf_op jit(solution)/shard_map/cond/branch_1_fun/ppermute | solution.py:486
  51.5 3.4 %copy-start.10 = (f32[384,512]{1,0:T(8,128)S(1)}, f32[384,512]{1,0:T(8,128)}, u32[]{:S(2)}) copy-start(f32[384,512]{1,0:T(8,128)} %copy-done.9) | copy-start | bytes 2359300 | tf_op jit(solution)/shard_map/cond
  51.5 11.8 %collective-permute-start.28 = (f32[10,32,256]{2,1,0:T(8,128)S(1)}, f32[10,32,256]{2,1,0:T(8,128)S(1)}, u32[]{:S(2)}, u32[]{:S(2)}) collective-permute-start(f32[10,32,256]{2,1,0:T(8,128)S(1)} %collective-permute-done.25.refs_0_.refs_6_), channel_id=1, source_target_pairs={{0,4},{4,0},{8,12},{12,8},{16,20},{20,16},{24,28},{28,24},{1,5},{5... | collective-permute-start | bytes 983048 | tf_op jit(solution)/shard_map/cond/branch_1_fun/ppermute | solution.py:461
  53.0 10.3 %collective-permute-start.27 = (f32[10,32,256]{2,1,0:T(8,128)S(1)}, f32[10,32,256]{2,1,0:T(8,128)S(1)}, u32[]{:S(2)}, u32[]{:S(2)}) collective-permute-start(f32[10,32,256]{2,1,0:T(8,128)S(1)} %branch_1_fun.7.refs_0_), channel_id=1, source_target_pairs={{0,8},{4,12},{8,16},{12,20},{16,24},{20,28},{24,0},{28,4},{1,9},{5... | collective-permute-start | bytes 983048 | tf_op jit(solution)/shard_map/cond/branch_1_fun/ppermute | solution.py:475
  54.9 19.3 %collective-permute-start.33 = (f32[2,10,32,256]{3,2,1,0:T(8,128)S(1)}, f32[2,10,32,256]{3,2,1,0:T(8,128)S(1)}, u32[]{:S(2)}, u32[]{:S(2)}) collective-permute-start(f32[2,10,32,256]{3,2,1,0:T(8,128)S(1)} %pad_maximum_fusion.3), channel_id=1, source_target_pairs={{0,1},{1,0},{2,3},{3,2},{4,5},{5,4},{6,7},{7,6},{8,9},{9,8},{10,11... | collective-permute-start | bytes 1966088 | tf_op jit(solution)/shard_map/cond/branch_1_fun/ppermute | solution.py:461
  59.7 7.8 %collective-permute-start.31 = (f32[6,32,256]{2,1,0:T(8,128)S(1)}, f32[6,32,256]{2,1,0:T(8,128)S(1)}, u32[]{:S(2)}, u32[]{:S(2)}) collective-permute-start(f32[6,32,256]{2,1,0:T(8,128)S(1)} %get-tuple-element.129), channel_id=1, source_target_pairs={{0,4},{4,0},{8,12},{12,8},{16,20},{20,16},{24,28},{28,24},{1,5},{5... | collective-permute-start | bytes 589832 | tf_op jit(solution)/shard_map/cond/branch_1_fun/ppermute | solution.py:461
  60.4 13.7 %collective-permute-start.34 = (f32[2,10,32,256]{3,2,1,0:T(8,128)S(1)}, f32[2,10,32,256]{3,2,1,0:T(8,128)S(1)}, u32[]{:S(2)}, u32[]{:S(2)}) collective-permute-start(f32[2,10,32,256]{3,2,1,0:T(8,128)S(1)} %pad_maximum_fusion.4), channel_id=1, source_target_pairs={{0,1},{1,0},{2,3},{3,2},{4,5},{5,4},{6,7},{7,6},{8,9},{9,8},{10,11... | collective-permute-start | bytes 1966088 | tf_op jit(solution)/shard_map/cond/branch_1_fun/ppermute | solution.py:461
  63.3 4.2 %collective-permute-start.30 = (f32[6,32,256]{2,1,0:T(8,128)S(1)}, f32[6,32,256]{2,1,0:T(8,128)S(1)}, u32[]{:S(2)}, u32[]{:S(2)}) collective-permute-start(f32[6,32,256]{2,1,0:T(8,128)S(1)} %get-tuple-element.130.refs_0_), channel_id=1, source_target_pairs={{0,1},{1,0},{2,3},{3,2},{4,5},{5,4},{6,7},{7,6},{8,9},{9,8},{10,11... | collective-permute-start | bytes 589832 | tf_op jit(solution)/shard_map/cond/branch_1_fun/ppermute | solution.py:461
  63.3 10.8 %collective-permute-start.29 = (f32[10,32,256]{2,1,0:T(8,128)S(1)}, f32[10,32,256]{2,1,0:T(8,128)S(1)}, u32[]{:S(2)}, u32[]{:S(2)}) collective-permute-start(f32[10,32,256]{2,1,0:T(8,128)S(1)} %collective-permute-done.27.refs_9_), channel_id=1, source_target_pairs={{0,4},{4,0},{8,12},{12,8},{16,20},{20,16},{24,28},{28,24},{1,5},{5... | collective-permute-start | bytes 983048 | tf_op jit(solution)/shard_map/cond/branch_1_fun/ppermute | solution.py:461
  67.5 6.7 %collective-permute-start.35 = (f32[2,10,32,256]{3,2,1,0:T(8,128)S(1)}, f32[2,10,32,256]{3,2,1,0:T(8,128)S(1)}, u32[]{:S(2)}, u32[]{:S(2)}) collective-permute-start(f32[2,10,32,256]{3,2,1,0:T(8,128)S(1)} %pad_maximum_fusion.5), channel_id=1, source_target_pairs={{0,1},{1,0},{2,3},{3,2},{4,5},{5,4},{6,7},{7,6},{8,9},{9,8},{10,11... | collective-permute-start | bytes 1966088 | tf_op jit(solution)/shard_map/cond/branch_1_fun/ppermute | solution.py:461
  67.5 2.4 %collective-permute-start.32 = (f32[6,32,256]{2,1,0:T(8,128)S(1)}, f32[6,32,256]{2,1,0:T(8,128)S(1)}, u32[]{:S(2)}, u32[]{:S(2)}) collective-permute-start(f32[6,32,256]{2,1,0:T(8,128)S(1)} %collective-permute-done.31.refs_2_), channel_id=1, source_target_pairs={{0,1},{1,0},{2,3},{3,2},{4,5},{5,4},{6,7},{7,6},{8,9},{9,8},{10,11... | collective-permute-start | bytes 589832 | tf_op jit(solution)/shard_map/cond/branch_1_fun/ppermute | solution.py:461
  69.9 4.3 %collective-permute-start.36 = (f32[10,32,256]{2,1,0:T(8,128)S(1)}, f32[10,32,256]{2,1,0:T(8,128)S(1)}, u32[]{:S(2)}, u32[]{:S(2)}) collective-permute-start(f32[10,32,256]{2,1,0:T(8,128)S(1)} %collective-permute-done.27.refs_9_), channel_id=1, source_target_pairs={{0,1},{1,0},{2,3},{3,2},{4,5},{5,4},{6,7},{7,6},{8,9},{9,8},{10,11... | collective-permute-start | bytes 983048 | tf_op jit(solution)/shard_map/cond/branch_1_fun/ppermute | solution.py:461
  74.1 1.6 %collective-permute-start.37 = (f32[10,32,256]{2,1,0:T(8,128)S(1)}, f32[10,32,256]{2,1,0:T(8,128)S(1)}, u32[]{:S(2)}, u32[]{:S(2)}) collective-permute-start(f32[10,32,256]{2,1,0:T(8,128)S(1)} %collective-permute-done.29.refs_10_), channel_id=1, source_target_pairs={{0,1},{1,0},{2,3},{3,2},{4,5},{5,4},{6,7},{7,6},{8,9},{9,8},{10,11... | collective-permute-start | bytes 983048 | tf_op jit(solution)/shard_map/cond/branch_1_fun/ppermute | solution.py:461
  79.4 0.9 %copy-start.1 = (f32[64,512]{1,0:T(8,128)S(1)}, f32[64,512]{1,0:T(8,128)}, u32[]{:S(2)}) copy-start(f32[64,512]{1,0:T(8,128)} %param.8) | copy-start | bytes 393220
